TPU v7x, 512 devices: a whole 4x8x8 slice. The times are simulated.
512 devices in a mesh: segment: 4 (over x), patch: 128 (over z, y, core).
Axes of the slice: x: 4, y: 8, z: 8, core: 2. Of those that a mesh axis runs over, the one named last changes fastest.
Arguments:
- x_in: bfloat16 [8192, 1536], P('patch'), may hold values from -6 to 6
- stale_kv: bfloat16 [4, 8192, 1536], P('segment', 'patch'), may hold values from -6 to 6
- owner: int32 [32, 16], replicated, may hold values from 0 to 15, each once within a row
- live: int32 [128], P('patch'), may hold values from 1 to 4, as said below
- gain: float32 [4, 1536], P('segment'), may hold values from 0.5 to 1.5
- qk_gain: float32 [4, 2, 64], P('segment'), may hold values from 0.5 to 1.5
- w_qkv: bfloat16 [4, 1536, 2304], P('segment', 'patch'), may hold values from -0.15625 to 0.15625
- w_out: bfloat16 [4, 768, 1536], P('segment', None, 'patch'), may hold values from -0.875 to 0.875
Outputs:
- sections: bfloat16 [4, 8192, 1536], P('segment', 'patch')
Inputs may be any that keep to these rules, and one draw needn't show every extreme that they name: `live`: every device denoises its first one or more micro-patches, and some device all 4. `owner`: each row holds every patch number of one image once.
All inputs are finite; a program needn't handle non-finite values.
Results may differ from a plain program's by a relative error of at most 0.023.
Values may be sent and summed in bfloat16 or wider, within the bound.
A program may use at most 64 MiB of HBM per device.

v0:
```python
import jax
import jax.numpy as jnp
from jax import lax
from jax.sharding import PartitionSpec as P

HEADS = 12
MICRO = 4
LEVELS = 2


def partner_2(value, axis, bit):
    mask = 2**bit
    pairs = [(source, source ^ mask) for source in range(lax.axis_size(axis))]
    return lax.ppermute(value, axis, pairs)


def from_behind(block, axis, distance):
    devices = range(lax.axis_size(axis))
    route = [(i - distance, i) for i in devices if i - distance in devices]
    return lax.ppermute(block, axis, route)


def scaled_rms(values, gain_row):
    return values * lax.rsqrt(jnp.mean(values * values, -1, keepdims=True) + 1e-06) * gain_row


def run_section(
    current,
    gain_row,
    head_gains,
    w_in,
    w_back,
    stale_keys,
    stale_vals,
    key_patch,
    patch_id,
    head_count,
):
    attn_width = w_back.shape[0]
    head_size = attn_width // head_count
    micro_rows = current.shape[0]
    widened = current.astype(jnp.float32)
    normed = scaled_rms(widened, gain_row).astype(jnp.bfloat16)
    fresh_rows = jnp.dot(normed, w_in, preferred_element_type=jnp.float32).astype(jnp.bfloat16)
    query_part = (
        fresh_rows[:, :attn_width].astype(jnp.float32).reshape(micro_rows, head_count, head_size)
    )
    key_part = (
        fresh_rows[:, attn_width : 2 * attn_width]
        .astype(jnp.float32)
        .reshape(micro_rows, head_count, head_size)
    )
    queries = scaled_rms(query_part, head_gains[0]).astype(jnp.bfloat16)
    own_keys = scaled_rms(key_part, head_gains[1]).astype(jnp.bfloat16)
    own_vals = fresh_rows[:, 2 * attn_width :].reshape(micro_rows, head_count, head_size)
    score_scale = head_size ** (-0.5)
    far_scores = (
        jnp.einsum("qhd,khd->hqk", queries, stale_keys, preferred_element_type=jnp.float32)
        * score_scale
    )
    far_exp = jnp.where(key_patch[None, None, :] == patch_id, jnp.float32(0.0), jnp.exp(far_scores))
    own_scores = (
        jnp.einsum("qhd,khd->hqk", queries, own_keys, preferred_element_type=jnp.float32)
        * score_scale
    )
    own_exp = jnp.exp(own_scores)
    row_total = far_exp.sum(-1) + own_exp.sum(-1)
    weighted = jnp.einsum(
        "hqk,khd->qhd", far_exp.astype(jnp.bfloat16), stale_vals, preferred_element_type=jnp.float32
    )
    weighted = weighted + jnp.einsum(
        "hqk,khd->qhd", own_exp.astype(jnp.bfloat16), own_vals, preferred_element_type=jnp.float32
    )
    attended = (
        (weighted / row_total.T[:, :, None]).reshape(micro_rows, attn_width).astype(jnp.bfloat16)
    )
    projected = jnp.dot(attended, w_back, preferred_element_type=jnp.float32)
    return (widened + projected).astype(jnp.bfloat16)


def per_device(x_in, stale_kv, owner, live, gain, qk_gain, w_qkv, w_out):
    w_in = lax.all_gather(w_qkv[0], "patch", axis=0, tiled=True)
    w_back = lax.all_gather(w_out[0], "patch", axis=1, tiled=True)
    level_count = LEVELS
    group_size = 2**level_count
    micro_count = MICRO
    patch_index = lax.axis_index("patch")
    position = patch_index % group_size
    image = patch_index // group_size
    context = stale_kv[0]
    labels = jnp.reshape(position, (1,))
    bit_order = list(range(level_count))
    for bit in bit_order:
        partner = partner_2(context, "patch", bit)
        mine_low = patch_index // 2**bit % 2 == 0
        lower = jnp.where(mine_low, context, partner)
        upper = jnp.where(mine_low, partner, context)
        context = jnp.concatenate([lower, upper], 0)
        partner_labels = labels + jnp.where(mine_low, 2**bit, -(2**bit)).astype(jnp.int32)
        lower_labels = jnp.where(mine_low, labels, partner_labels)
        upper_labels = jnp.where(mine_low, partner_labels, labels)
        labels = jnp.concatenate([lower_labels, upper_labels], 0)
    head_count = HEADS
    attn_width = w_back.shape[0]
    head_size = attn_width // head_count
    context_rows = context.shape[0]
    device_rows = x_in.shape[0]
    micro_rows = device_rows // micro_count
    stale_keys = context[:, :attn_width].reshape(context_rows, head_count, head_size)
    stale_vals = context[:, attn_width:].reshape(context_rows, head_count, head_size)
    row_patch = lax.iota(jnp.int32, device_rows) // micro_rows
    key_patch = (labels[:, None] * micro_count + row_patch[None, :]).reshape(context_rows)
    owner_row = lax.dynamic_slice(owner, (image, position * micro_count), (1, micro_count))[0]
    live_count = live[0]
    gain_row = gain[0]
    head_gains = qk_gain[0]
    segment_index = lax.axis_index("segment")
    segment_count = lax.axis_size("segment")
    turns = micro_count + segment_count - 1
    carried = jnp.zeros((micro_rows, x_in.shape[1]), jnp.bfloat16)
    outputs = jnp.zeros_like(x_in)
    for moment in range(turns):
        micro_index = moment - segment_index
        is_valid = (micro_index >= 0) & (micro_index < micro_count)
        clipped = jnp.clip(micro_index, 0, micro_count - 1)
        first_row = clipped * micro_rows
        from_input = lax.dynamic_slice_in_dim(x_in, first_row, micro_rows, 0)
        current = jnp.where(segment_index == 0, from_input, carried)
        do_work = is_valid & (clipped < live_count)
        patch_id = owner_row[clipped]

        def working(block):
            return run_section(
                block,
                gain_row,
                head_gains,
                w_in,
                w_back,
                stale_keys,
                stale_vals,
                key_patch,
                patch_id,
                head_count,
            )

        def passing(block):
            return block

        result = lax.cond(do_work, working, passing, current)
        updated = lax.dynamic_update_slice_in_dim(outputs, result, first_row, 0)
        outputs = jnp.where(is_valid, updated, outputs)
        if moment + 1 < turns:
            carried = from_behind(result, "segment", 1)
    return outputs[None]


def solution(mesh):
    in_specs = (
        P("patch", None),
        P("segment", "patch", None),
        P(),
        P("patch"),
        P("segment", None),
        P("segment", None, None),
        P("segment", "patch", None),
        P("segment", None, "patch"),
    )
    out_specs = P("segment", "patch", None)
    return jax.shard_map(
        per_device, mesh=mesh, in_specs=in_specs, out_specs=out_specs, check_vma=False
    )
```

profile of v0, /device:TPU:14, one launch (start us, length us, event | category | flops | bytes accessed | tf_op | source)
XLA Modules:
  0.0 363.2 jit_solution(16511205159057156927)
XLA Ops:
  8.0 1.6 copy.180
  9.6 1.9 collective-permute-start
  14.2 2.4 collective-permute-start.1
  17.4 9.8 %collective-permute-done.1 = bf16[128,1536]{1,0:T(8,128)(2,1)S(1)} collective-permute-done((bf16[128,1536]{1,0:T(8,128)(2,1)S(1)}, bf16[128,1536]{1,0:T(8,128)(2,1)S(1)}, u32[]{:S(2)}, u32[]{:S(2)}) %collective-permute-start.1) | collective-permute-done | bytes 393248 | tf_op jit(solution)/shard_map/ppermute | solution.py:14
  27.8 72.0 %all-gather.7.cloned.1.call-done = bf16[1,768,1536]{1,0,2:T(2,128)(2,1)} async-done(((bf16[1,768,12]{1,0,2:T(2,128)(2,1)}), bf16[1,768,1536]{1,0,2:T(2,128)(2,1)}) %all-gather.7.cloned.1.call-update) | async-done | bytes 2359312 | tf_op jit(solution)/shard_map/all_gather | solution.py:83
  99.7 10.1 %copy.184 = bf16[1,768,1536]{2,1,0:T(8,128)(2,1)S(1)} copy(bf16[1,768,1536]{1,0,2:T(2,128)(2,1)} %all-gather.7.cloned.1.call-done) | data formatting | bytes 4718592 | tf_op jit(solution)/shard_map/all_gather | solution.py:83
  109.9 84.7 %all-gather.5.cloned.1.call-done = bf16[1,1536,2304]{2,0,1:T(2,128)(2,1)} async-done(((bf16[1,12,2304]{2,0,1:T(2,128)(2,1)}), bf16[1,1536,2304]{2,0,1:T(2,128)(2,1)}) %all-gather.5.cloned.1.call-update) | async-done | bytes 7077904 | tf_op jit(solution)/shard_map/all_gather | solution.py:82
  194.5 9.0 %copy.292 = bf16[1,1536,2304]{2,1,0:T(8,128)(2,1)} copy(bf16[1,1536,2304]{2,0,1:T(2,128)(2,1)} %all-gather.5.cloned.1.call-done) | data formatting | bytes 14155776
  204.9 4.6 %collective-permute-done.2 = bf16[16,1536]{1,0:T(8,128)(2,1)S(1)} collective-permute-done((bf16[16,1536]{1,0:T(8,128)(2,1)S(1)}, bf16[16,1536]{1,0:T(8,128)(2,1)S(1)}, u32[]{:S(2)}, u32[]{:S(2)}) %collective-permute-start.2) | collective-permute-done | bytes 49184 | tf_op jit(solution)/shard_map/ppermute | solution.py:20
  211.7 4.7 %collective-permute-done.3 = bf16[16,1536]{1,0:T(8,128)(2,1)S(1)} collective-permute-done((bf16[16,1536]{1,0:T(8,128)(2,1)S(1)}, bf16[16,1536]{1,0:T(8,128)(2,1)S(1)}, u32[]{:S(2)}, u32[]{:S(2)}) %collective-permute-start.3) | collective-permute-done | bytes 49184 | tf_op jit(solution)/shard_map/ppermute | solution.py:20
  218.5 46.6 %collective-permute-done.4 = bf16[16,1536]{1,0:T(8,128)(2,1)S(1)} collective-permute-done((bf16[16,1536]{1,0:T(8,128)(2,1)S(1)}, bf16[16,1536]{1,0:T(8,128)(2,1)S(1)}, u32[]{:S(2)}, u32[]{:S(2)}) %collective-permute-start.4) | collective-permute-done | bytes 49184 | tf_op jit(solution)/shard_map/ppermute | solution.py:20
  265.8 17.7 %conditional.10 = (bf16[16,1536]{1,0:T(8,128)(2,1)S(1)}) conditional(s32[]{:T(128)} %convert_element_type.248, bf16[16,1536]{1,0:T(8,128)(2,1)S(1)} %dynamic-slice_select_fusion.3, (bf16[16,1536]{1,0:T(8,128)(2,1)S(1)}, s32[]{:T(128)}, s32[]{:T(128)}, s32[32,16]{0,1:T(8,128)}, s32[]{:T(128)}, /*index=5*/s32[4,64]{1,0:T(4,128)S(1)}, ...), branch_computations={%region_21.22_spmd, %region_22.28_spmd} | conditional | flops 165037520 | bytes 11768120 | solution.py:149
  266.0 4.1 %convolution_convert_fusion.3 = bf16[16,2304]{1,0:T(8,128)(2,1)S(1)} fusion(bf16[1536,2304]{1,0:T(8,128)(2,1)} %get-tuple-element.286, bf16[16,1536]{1,0:T(8,128)(2,1)S(1)} %get-tuple-element.279, f32[1536]{0:T(1024)S(1)} %reduce.3, f32[16]{0:T(128)S(1)} %add_rsqrt_fusion.11), kind=kOutput, calls=%fused_computation.117 | convolution fusion | flops 113381376 | bytes 7206976 | tf_op jit(solution)/shard_map/cond/branch_1_fun/dot_general | solution.py:44
  271.8 1.5 reshape.450
  274.4 1.7 multiply_convert_fusion.6
  279.4 1.5 reshape.413
  284.8 4.7 %collective-permute-done.5 = bf16[16,1536]{1,0:T(8,128)(2,1)S(1)} collective-permute-done((bf16[16,1536]{1,0:T(8,128)(2,1)S(1)}, bf16[16,1536]{1,0:T(8,128)(2,1)S(1)}, u32[]{:S(2)}, u32[]{:S(2)}) %collective-permute-start.5) | collective-permute-done | bytes 49184 | tf_op jit(solution)/shard_map/ppermute | solution.py:20
  290.3 17.8 %conditional.11 = (bf16[16,1536]{1,0:T(8,128)(2,1)S(1)}) conditional(s32[]{:T(128)} %convert_element_type.249, bf16[16,1536]{1,0:T(8,128)(2,1)S(1)} %dynamic-slice_select_fusion.2, (bf16[16,1536]{1,0:T(8,128)(2,1)S(1)}, s32[]{:T(128)}, s32[]{:T(128)}, s32[32,16]{0,1:T(8,128)}, s32[]{:T(128)}, /*index=5*/s32[4,64]{1,0:T(4,128)S(1)}, ...), branch_computations={%region_28.29_spmd, %region_29.35_spmd} | conditional | flops 165037520 | bytes 11768120 | solution.py:149
  290.7 4.1 %convolution_convert_fusion.4 = bf16[16,2304]{1,0:T(8,128)(2,1)S(1)} fusion(bf16[1536,2304]{1,0:T(8,128)(2,1)} %get-tuple-element.298, bf16[16,1536]{1,0:T(8,128)(2,1)S(1)} %get-tuple-element.291, f32[1536]{0:T(1024)S(1)} %reduce.4, f32[16]{0:T(128)S(1)} %add_rsqrt_fusion.14), kind=kOutput, calls=%fused_computation.156 | convolution fusion | flops 113381376 | bytes 7206976 | tf_op jit(solution)/shard_map/cond/branch_1_fun/dot_general | solution.py:44
  296.4 1.5 reshape.454
  299.0 1.7 multiply_convert_fusion.8
  304.0 1.5 reshape.418
  309.5 4.7 %collective-permute-done.6 = bf16[16,1536]{1,0:T(8,128)(2,1)S(1)} collective-permute-done((bf16[16,1536]{1,0:T(8,128)(2,1)S(1)}, bf16[16,1536]{1,0:T(8,128)(2,1)S(1)}, u32[]{:S(2)}, u32[]{:S(2)}) %collective-permute-start.6) | collective-permute-done | bytes 49184 | tf_op jit(solution)/shard_map/ppermute | solution.py:20
  315.0 17.7 %conditional.12 = (bf16[16,1536]{1,0:T(8,128)(2,1)S(1)}) conditional(s32[]{:T(128)} %convert_element_type.250, bf16[16,1536]{1,0:T(8,128)(2,1)S(1)} %dynamic-slice_select_fusion.1, (bf16[16,1536]{1,0:T(8,128)(2,1)S(1)}, s32[]{:T(128)}, s32[]{:T(128)}, s32[32,16]{0,1:T(8,128)}, s32[]{:T(128)}, /*index=5*/s32[4,64]{1,0:T(4,128)S(1)}, ...), branch_computations={%region_35.36_spmd, %region_36.42_spmd} | conditional | flops 165037520 | bytes 11768120 | solution.py:149
  315.1 4.1 %convolution_convert_fusion.5 = bf16[16,2304]{1,0:T(8,128)(2,1)S(1)} fusion(bf16[1536,2304]{1,0:T(8,128)(2,1)} %get-tuple-element.310, bf16[16,1536]{1,0:T(8,128)(2,1)S(1)} %get-tuple-element.303, f32[1536]{0:T(1024)S(1)} %reduce.5, f32[16]{0:T(128)S(1)} %add_rsqrt_fusion.17), kind=kOutput, calls=%fused_computation.195 | convolution fusion | flops 113381376 | bytes 7206976 | tf_op jit(solution)/shard_map/cond/branch_1_fun/dot_general | solution.py:44
  320.9 1.5 reshape.458
  323.5 1.7 multiply_convert_fusion.10
  334.6 4.0 %collective-permute-done.7 = bf16[16,1536]{1,0:T(8,128)(2,1)S(1)} collective-permute-done((bf16[16,1536]{1,0:T(8,128)(2,1)S(1)}, bf16[16,1536]{1,0:T(8,128)(2,1)S(1)}, u32[]{:S(2)}, u32[]{:S(2)}) %collective-permute-start.7) | collective-permute-done | bytes 49184 | tf_op jit(solution)/shard_map/ppermute | solution.py:20
  339.4 16.3 %conditional.13 = (bf16[16,1536]{1,0:T(8,128)(2,1)S(1)}) conditional(s32[]{:T(128)} %convert_element_type.251, bf16[16,1536]{1,0:T(8,128)(2,1)S(1)} %dynamic-slice_select_fusion, (bf16[16,1536]{1,0:T(8,128)(2,1)S(1)}, s32[]{:T(128)}, s32[]{:T(128)}, s32[32,16]{0,1:T(8,128)}, s32[]{:T(128)}, /*index=5*/s32[4,64]{1,0:T(4,128)S(1)}, ...), branch_computations={%region_42.43_spmd, %region_43.49_spmd} | conditional | flops 165037520 | bytes 11768120 | solution.py:149
  339.6 4.1 %convolution_convert_fusion.6 = bf16[16,2304]{1,0:T(8,128)(2,1)S(1)} fusion(bf16[1536,2304]{1,0:T(8,128)(2,1)} %get-tuple-element.322, bf16[16,1536]{1,0:T(8,128)(2,1)S(1)} %get-tuple-element.315, f32[1536]{0:T(1024)S(1)} %reduce.6, f32[16]{0:T(128)S(1)} %add_rsqrt_fusion.20), kind=kOutput, calls=%fused_computation.234 | convolution fusion | flops 113381376 | bytes 7206976 | tf_op jit(solution)/shard_map/cond/branch_1_fun/dot_general | solution.py:44
  345.4 1.5 reshape.462
  347.9 1.7 multiply_convert_fusion.12
  (131 shorter events, 55.4 us)
Async XLA Ops:
  6.5 93.2 %all-gather.7.cloned.1.call-start = ((), (), s32[]{:S(2)}) async-start(), calls=%async_computation.1 | async-start | bytes 4755456 | tf_op jit(solution)/shard_map/all_gather | solution.py:83
  7.9 186.6 %all-gather.5.cloned.1.call-start = ((), (), s32[]{:S(2)}) async-start(), calls=%async_computation | async-start | bytes 14266368 | tf_op jit(solution)/shard_map/all_gather | solution.py:82
  9.6 3.5 collective-permute-start
  14.2 13.1 %collective-permute-start.1 = (bf16[128,1536]{1,0:T(8,128)(2,1)S(1)}, bf16[128,1536]{1,0:T(8,128)(2,1)S(1)}, u32[]{:S(2)}, u32[]{:S(2)}) collective-permute-start(bf16[128,1536]{1,0:T(8,128)(2,1)S(1)} %pad_maximum_fusion.1), channel_id=1, source_target_pairs={{0,2},{1,3},{2,0},{3,1},{4,6},{5,7},{6,4},{7,5},{8,10},{9,11},{10,... | collective-permute-start | bytes 1179656 | tf_op jit(solution)/shard_map/ppermute | solution.py:14
  109.8 93.7 %copy-start = (f32[1,1536]{1,0:T(1,128)S(1)}, f32[1,1536]{1,0:T(1,128)}, u32[]{:S(2)}) copy-start(f32[1,1536]{1,0:T(1,128)} %param.26) | copy-start | bytes 18436
  109.8 93.7 %copy-start.1 = (f32[1,2,64]{2,1,0:T(2,128)S(1)}, f32[1,2,64]{2,1,0:T(2,128)}, u32[]{:S(2)}) copy-start(f32[1,2,64]{2,1,0:T(2,128)} %param.27) | copy-start | bytes 1540
  203.5 6.0 %collective-permute-start.2 = (bf16[16,1536]{1,0:T(8,128)(2,1)S(1)}, bf16[16,1536]{1,0:T(8,128)(2,1)S(1)}, u32[]{:S(2)}, u32[]{:S(2)}) collective-permute-start(bf16[16,1536]{1,0:T(8,128)(2,1)S(1)} %get-tuple-element.524), channel_id=1, source_target_pairs={{0,128},{128,256},{256,384},{1,129},{129,257},{257,385},{2,130},{1... | collective-permute-start | bytes 147464 | tf_op jit(solution)/shard_map/ppermute | solution.py:20
  210.3 6.0 %collective-permute-start.3 = (bf16[16,1536]{1,0:T(8,128)(2,1)S(1)}, bf16[16,1536]{1,0:T(8,128)(2,1)S(1)}, u32[]{:S(2)}, u32[]{:S(2)}) collective-permute-start(bf16[16,1536]{1,0:T(8,128)(2,1)S(1)} %get-tuple-element.525), channel_id=1, source_target_pairs={{0,128},{128,256},{256,384},{1,129},{129,257},{257,385},{2,130},{1... | collective-permute-start | bytes 147464 | tf_op jit(solution)/shard_map/ppermute | solution.py:20
  217.2 47.9 %collective-permute-start.4 = (bf16[16,1536]{1,0:T(8,128)(2,1)S(1)}, bf16[16,1536]{1,0:T(8,128)(2,1)S(1)}, u32[]{:S(2)}, u32[]{:S(2)}) collective-permute-start(bf16[16,1536]{1,0:T(8,128)(2,1)S(1)} %get-tuple-element.526), channel_id=1, source_target_pairs={{0,128},{128,256},{256,384},{1,129},{129,257},{257,385},{2,130},{1... | collective-permute-start | bytes 147464 | tf_op jit(solution)/shard_map/ppermute | solution.py:20
  283.5 6.0 %collective-permute-start.5 = (bf16[16,1536]{1,0:T(8,128)(2,1)S(1)}, bf16[16,1536]{1,0:T(8,128)(2,1)S(1)}, u32[]{:S(2)}, u32[]{:S(2)}) collective-permute-start(bf16[16,1536]{1,0:T(8,128)(2,1)S(1)} %get-tuple-element.527), channel_id=1, source_target_pairs={{0,128},{128,256},{256,384},{1,129},{129,257},{257,385},{2,130},{1... | collective-permute-start | bytes 147464 | tf_op jit(solution)/shard_map/ppermute | solution.py:20
  308.2 6.0 %collective-permute-start.6 = (bf16[16,1536]{1,0:T(8,128)(2,1)S(1)}, bf16[16,1536]{1,0:T(8,128)(2,1)S(1)}, u32[]{:S(2)}, u32[]{:S(2)}) collective-permute-start(bf16[16,1536]{1,0:T(8,128)(2,1)S(1)} %get-tuple-element.528), channel_id=1, source_target_pairs={{0,128},{128,256},{256,384},{1,129},{129,257},{257,385},{2,130},{1... | collective-permute-start | bytes 147464 | tf_op jit(solution)/shard_map/ppermute | solution.py:20
  332.6 6.0 %collective-permute-start.7 = (bf16[16,1536]{1,0:T(8,128)(2,1)S(1)}, bf16[16,1536]{1,0:T(8,128)(2,1)S(1)}, u32[]{:S(2)}, u32[]{:S(2)}) collective-permute-start(bf16[16,1536]{1,0:T(8,128)(2,1)S(1)} %get-tuple-element.529), channel_id=1, source_target_pairs={{0,128},{128,256},{256,384},{1,129},{129,257},{257,385},{2,130},{1... | collective-permute-start | bytes 147464 | tf_op jit(solution)/shard_map/ppermute | solution.py:20
Sparse Core Ops, SparseCore 0:
  10.6 89.1 all-gather.6
  102.9 91.5 all-gather.4
where the time goes:
time: 366 us; the launch traced here: 363 us
  waiting for transfers between devices  236 us (64%)
  local copies, waits for them, and re-layouts  44.1 us (12%)
  matrix products  30.7 us (8%)
  other arithmetic  25 us (7%)
  between operations  14.4 us (4%)
  starting transfers between devices  12.1 us (3%)
    all_gather x1, waiting for transfers between devices, per_device(): w_in = lax.all_gather(w_qkv[0], 'patch', axis=0, tiled=True)  84.7 us
    all_gather x1, waiting for transfers between devices, per_device(): w_back = lax.all_gather(w_out[0], 'patch', axis=1, tiled=True)  72 us
    ppermute x6, waiting for transfers between devices, from_behind(): return lax.ppermute(block, axis, route)  69.1 us
    dot_general x4, matrix products, run_section(): jnp.dot(normed, w_in, preferred_element_type=jnp.float32)  16.3 us
    unnamed x8, local copies, waits for them, and re-layouts  12.7 us
    ppermute x2, waiting for transfers between devices, partner_2(): return lax.ppermute(value, axis, pairs)  10.5 us
    all_gather x1, local copies, waits for them, and re-layouts, per_device(): w_back = lax.all_gather(w_out[0], 'patch', axis=1, tiled=True)  10.1 us
    ppermute x6, starting transfers between devices, from_behind(): return lax.ppermute(block, axis, route)  7.73 us
  transfers between devices with their start and end apart: 10, of which 10 were waited for; matrix products, arithmetic and copies ran while one was open for 4% of the time, Pallas kernels for 0%

commit v1 on v0

v1 whole, which is shorter than its diff:
```python
import functools

import jax
import jax.numpy as jnp
from jax import lax
from jax.experimental import pallas as pl
from jax.experimental.pallas import tpu as pltpu
from jax.sharding import PartitionSpec as P

MESH = pl.DeviceIdType.MESH
BF = jnp.bfloat16
F32 = jnp.float32

SEG = 4
NZ = 8
NY = 8
GROUP = 4
SHARD = 12
SLOT = 16
BLOCK = GROUP * SHARD
ROWS = 64
MROWS = 16
MICRO = 4
IMG = GROUP * ROWS
HEAD = 64
GH = 3
GW = GH * HEAD
PIECE = 2 * GW
D = 1536
HD = 768
LONG = NZ // 2
SHORT = NZ - 1 - LONG


def kernel(
    x_ref, stale_ref, owner_ref, live_ref, gain_ref, qkg_ref, wqkv_ref, wout_ref,
    out_ref,
    wsend, stg, blk, w, stsend, st, gains, qkgs, xs, rs_out, rs_in, own_part,
    wst_s, wst_r, g_s, g_r, qg_s, qg_r, st_s, st_r, y_s, y_r,
    rl_s, rl_r, sh_s, sh_r, m_s, m_r, rs_s, rs_r, ag_s, ag_r, loc,
):
    c = lax.axis_index("segment")
    p = lax.axis_index("patch")
    image = p // GROUP
    j = p % GROUP
    core = p % 2
    y = (p // 2) % NY
    z = p // (2 * NY)
    yp = y // 2
    mate = p + 1 - 2 * core

    def dev(seg, patch):
        return (seg, patch)

    def patch_of(zz, yy, cc):
        return zz * (2 * NY) + yy * 2 + cc

    barrier = pltpu.get_barrier_semaphore()
    partners = []
    for dc in range(SEG):
        for dj in range(GROUP):
            if dc or dj:
                partners.append(dev((c + dc) % SEG, image * GROUP + (j + dj) % GROUP))
    for dy in range(1, NY // 2):
        pair = (yp + dy) % (NY // 2)
        for low in range(4):
            partners.append(dev(c, z * (2 * NY) + pair * 4 + low))
    step = 1 - 2 * core
    z_long = (z + step + NZ) % NZ
    z_short = (z - step + NZ) % NZ
    partners.append(dev(c, patch_of(z_long, y, core)))
    partners.append(dev(c, patch_of(z_short, y, core)))
    for partner in partners:
        pl.semaphore_signal(barrier, inc=1, device_id=partner, device_id_type=MESH)

    wsend[...] = jnp.zeros_like(wsend)
    for g in range(SEG):
        for part in range(3):
            wsend[g, 0:SHARD, part * GW : (part + 1) * GW] = wqkv_ref[
                :, part * HD + g * GW : part * HD + (g + 1) * GW
            ]
        wsend[g, 0:SHARD, 3 * GW :] = wout_ref[:, g * GW : (g + 1) * GW]
        for part in range(2):
            stsend[g, :, part * GW : (part + 1) * GW] = stale_ref[
                :, part * HD + g * GW : part * HD + (g + 1) * GW
            ]
    for g in range(SEG):
        xs[0, g] = x_ref[:, g * PIECE : (g + 1) * PIECE]
    gains[c] = gain_ref[...]
    qkgs[c] = qkg_ref[...]
    pl.semaphore_wait(barrier, len(partners))

    def remote(src, dst, ss, rs, device):
        return pltpu.make_async_remote_copy(
            src_ref=src, dst_ref=dst, send_sem=ss, recv_sem=rs,
            device_id=device, device_id_type=MESH,
        )

    def stage(d):
        g = (c + d) % SEG
        return remote(
            wsend.at[g], stg.at[j], wst_s.at[d], wst_r.at[j], dev(g, image * GROUP + c)
        )

    def stage_local():
        return pltpu.make_async_copy(wsend.at[c], stg.at[j], wst_r.at[j])

    for d in range(1, SEG):
        stage(d).start()

    @pl.when(j == c)
    def _():
        stage_local().start()

    @pl.when(j != c)
    def _():
        stage(0).start()

    def gain_copy(d):
        return remote(gain_ref, gains.at[c], g_s.at[d - 1], g_r.at[d - 1], dev((c + d) % SEG, p))

    def qkg_copy(d):
        return remote(qkg_ref, qkgs.at[c], qg_s.at[d - 1], qg_r.at[d - 1], dev((c + d) % SEG, p))

    for d in range(1, SEG):
        gain_copy(d).start()
        qkg_copy(d).start()

    def stale_copy(dc, dj):
        g = (c + dc) % SEG
        return remote(
            stsend.at[g], st.at[c, j], st_s.at[dc * GROUP + dj], st_r.at[c],
            dev(g, image * GROUP + (j + dj) % GROUP),
        )

    pltpu.make_async_copy(stsend.at[c], st.at[c, j], st_r.at[c]).start()
    for dj in range(GROUP):
        for dc in range(SEG):
            if dc or dj:
                stale_copy(dc, dj).start()

    for slot in range(GROUP):
        pltpu.make_async_copy(wsend.at[0], stg.at[slot], wst_r.at[slot]).wait()
    a = lax.broadcasted_iota(jnp.int32, (BLOCK, GROUP * SLOT), 0)
    b = lax.broadcasted_iota(jnp.int32, (BLOCK, GROUP * SLOT), 1)
    pick = jnp.zeros((BLOCK, GROUP * SLOT), F32)
    for slot in range(GROUP):
        hit = (a - SHARD * slot == b - SLOT * slot) & (b >= SLOT * slot) & (b < SLOT * slot + SHARD)
        pick = jnp.where(hit, 1.0, pick)
    packed = jnp.dot(
        pick.astype(BF), stg[...].reshape(GROUP * SLOT, 2 * PIECE), preferred_element_type=F32
    ).astype(BF)
    blk[0] = packed[:, :PIECE]
    blk[1] = packed[:, PIECE:]

    def y_copy(dy, piece):
        target = patch_of(z, (y + dy) % NY, piece)
        return remote(
            blk.at[piece], w.at[j, piece, z, yp], y_s.at[dy * 2 + piece], y_r.at[j], dev(c, target)
        )

    def y_mate():
        return remote(
            blk.at[1 - core], w.at[j, 1 - core, z, yp], y_s.at[0], y_r.at[j], dev(c, mate)
        )

    def y_start(s):
        @pl.when(j == s)
        def _():
            pltpu.make_async_copy(blk.at[core], w.at[j, core, z, yp], y_r.at[j]).start()
            y_mate().start()
            for dy in (1, 7, 2, 6, 3, 5, 4):
                for piece in range(2):
                    y_copy(dy, piece).start()

    def ring(s, t, way):
        if way == 0:
            source, target, ss, rs = z - step * t, z_long, rl_s, rl_r
        else:
            source, target, ss, rs = z + step * t, z_short, sh_s, sh_r
        block = w.at[s, core, (source + NZ) % NZ]
        return remote(block, block, ss.at[s, t], rs.at[s, t], dev(c, patch_of(target, y, core)))

    def to_mate(s, t, way):
        source = z - step * t if way == 0 else z + step * t
        block = w.at[s, core, (source + NZ) % NZ]
        index = t if way == 0 else LONG + t
        return remote(block, block, m_s.at[s, index], m_r.at[s], dev(c, mate))

    def ring_wait(s, t, way):
        source = z - step * t if way == 0 else z + step * t
        block = w.at[s, core, (source + NZ) % NZ]
        rs = rl_r if way == 0 else sh_r
        pltpu.make_async_copy(block, block, rs.at[s, t - 1]).wait()

    def ring_start(s):
        block = w.at[s, core, z]
        pltpu.make_async_copy(block, block, y_r.at[s]).wait()
        ring(s, 0, 0).start()
        ring(s, 0, 1).start()
        to_mate(s, 0, 0).start()

    def ring_round(s, t):
        for way, hops in ((0, LONG), (1, SHORT)):
            if t <= hops:
                ring_wait(s, t, way)
                if t < hops:
                    ring(s, t, way).start()
                to_mate(s, t, way).start()

    y_start(0)
    ring_start(0)
    y_start(1)
    ring_round(0, 1)
    y_start(2)
    ring_round(0, 2)
    y_start(3)
    ring_round(0, 3)
    ring_start(1)
    ring_round(0, 4)

    lane_g = lax.broadcasted_iota(jnp.int32, (1, GW), 1)
    head_of = [(lane_g >= h * HEAD) & (lane_g < (h + 1) * HEAD) for h in range(GH)]
    lane_w = lax.broadcasted_iota(jnp.int32, (1, 256), 1)
    head_in_window = [(lane_w >= 64 + h * HEAD) & (lane_w < 64 + (h + 1) * HEAD) for h in range(GH)]
    row = lax.broadcasted_iota(jnp.int32, (ROWS, IMG), 0)
    key_row = lax.broadcasted_iota(jnp.int32, (ROWS, IMG), 1)
    barred = jnp.zeros((ROWS, IMG), jnp.int32)
    live_count = live_ref[0]
    for m in range(MICRO):
        first = owner_ref[image, j * MICRO + m] * MROWS
        hit = (row >= m * MROWS) & (row < (m + 1) * MROWS) & (key_row >= first) & (key_row < first + MROWS)
        barred = jnp.where(hit, 1, barred)
    far_mask = jnp.where(barred == 1, 0.0, 1.0)
    far_mask = jnp.concatenate([far_mask] * GH, 0)
    own_r = lax.broadcasted_iota(jnp.int32, (ROWS, ROWS), 0)
    own_k = lax.broadcasted_iota(jnp.int32, (ROWS, ROWS), 1)
    own_mask = jnp.zeros((ROWS, ROWS), F32)
    for m in range(MICRO):
        lo, hi = m * MROWS, (m + 1) * MROWS
        own_mask = jnp.where((own_r >= lo) & (own_r < hi) & (own_k >= lo) & (own_k < hi), 1.0, own_mask)
    own_mask = jnp.concatenate([own_mask] * GH, 0)
    row1 = lax.broadcasted_iota(jnp.int32, (ROWS, 1), 0)
    live_rows = jnp.where(row1 < live_count * MROWS, 1.0, 0.0)
    live_rows = jnp.concatenate([live_rows] * GH, 0)

    def head_norm(part, gain_row):
        squares = part * part
        scale = jnp.zeros_like(part)
        for h in range(GH):
            mean = jnp.sum(jnp.where(head_of[h], squares, 0.0), -1, keepdims=True) * (1.0 / HEAD)
            scale = jnp.where(head_of[h], lax.rsqrt(mean + 1e-06), scale)
        return part * scale * gain_row

    def nt(lhs, rhs):
        return lax.dot_general(lhs, rhs, (((1,), (1,)), ((), ())), preferred_element_type=F32)

    def chain_front(s):
        other = 1 - core
        pltpu.make_async_copy(w.at[s, other], w.at[s, other], m_r.at[s]).wait()
        if s == 0:
            for d in range(1, SEG):
                src = (c + SEG - d) % SEG
                pltpu.make_async_copy(gain_ref, gains.at[src], g_r.at[d - 1]).wait()
                pltpu.make_async_copy(qkg_ref, qkgs.at[src], qg_r.at[d - 1]).wait()
        else:
            for d in range(1, SEG):
                src = (c + SEG - d) % SEG
                pltpu.make_async_copy(xs.at[s, src], xs.at[s, src], ag_r.at[s - 1, d - 1]).wait()
        x = jnp.concatenate([xs[s, g] for g in range(SEG)], 1).astype(F32)
        inverse = lax.rsqrt(jnp.mean(x * x, -1, keepdims=True) + 1e-06)
        normed = (x * inverse * gains[s]).astype(BF)
        qk = jnp.dot(normed, w[s, 0].reshape(D, PIECE), preferred_element_type=F32).astype(BF).astype(F32)
        value = jnp.dot(normed, w[s, 1].reshape(D, PIECE), preferred_element_type=F32).astype(BF)
        gq = qkgs[s, 0:1, :]
        gk = qkgs[s, 1:2, :]
        query = head_norm(qk[:, :GW], jnp.concatenate([gq] * GH, 1))
        key = head_norm(qk[:, GW:], jnp.concatenate([gk] * GH, 1)).astype(BF)
        query = query.astype(BF).astype(F32)
        stacked = jnp.concatenate([jnp.where(head_of[h], query, 0.0) for h in range(GH)], 0).astype(BF)
        pltpu.make_async_copy(st.at[s], st.at[s], st_r.at[s]).wait()
        kv = st[s].reshape(IMG, PIECE)
        scale = HEAD**-0.5
        far = jnp.exp(nt(stacked, kv[:, :GW]) * scale) * far_mask
        own = jnp.exp(nt(stacked, key) * scale) * own_mask
        total = jnp.sum(far, -1, keepdims=True) + jnp.sum(own, -1, keepdims=True)
        value_window = jnp.concatenate([jnp.zeros((ROWS, 64), F32), value[:, :GW].astype(F32)], 1).astype(BF)
        weighted = jnp.dot(far.astype(BF), kv[:, PIECE - 256 :], preferred_element_type=F32)
        weighted = weighted + jnp.dot(own.astype(BF), value_window, preferred_element_type=F32)
        weighted = weighted * (live_rows / total)
        attended = jnp.zeros((ROWS, 256), F32)
        for h in range(GH):
            attended = jnp.where(head_in_window[h], weighted[h * ROWS : (h + 1) * ROWS], attended)
        attended = attended.astype(BF)
        for d in (1, 2, 3, 0):
            g = (c + d) % SEG
            rows = w[s, 1, pl.ds(2 * g, 2), :, :, PIECE - 256 :].reshape(PIECE, 256)
            part = nt(attended, rows)
            if d:
                rs_out[s, d - 1] = part.astype(BF)
                rs_copy(s, d).start()
            else:
                own_part[...] = part

    def rs_copy(s, d):
        return remote(
            rs_out.at[s, d - 1], rs_in.at[s, d - 1], rs_s.at[s, d - 1], rs_r.at[s, d - 1],
            dev((c + d) % SEG, p),
        )

    def ag_copy(s, d):
        return remote(
            xs.at[s + 1, c], xs.at[s + 1, c], ag_s.at[s, d - 1], ag_r.at[s, d - 1],
            dev((c + d) % SEG, p),
        )

    def chain_back(s):
        for d in range(1, SEG):
            pltpu.make_async_copy(rs_in.at[s, d - 1], rs_in.at[s, d - 1], rs_r.at[s, d - 1]).wait()
        total = own_part[...]
        for d in range(1, SEG):
            total = total + rs_in[s, d - 1].astype(F32)
        xs[s + 1, c] = (xs[s, c].astype(F32) + total).astype(BF)
        for d in range(1, SEG):
            ag_copy(s, d).start()

    for s in range(SEG):
        chain_front(s)
        if s + 1 < SEG:
            ring_round(s + 1, 1)
        chain_back(s)
        if s + 1 < SEG:
            ring_round(s + 1, 2)
            ring_round(s + 1, 3)
            if s + 2 < SEG:
                ring_start(s + 2)
            ring_round(s + 1, 4)

    for d in range(1, SEG):
        src = (c + SEG - d) % SEG
        pltpu.make_async_copy(xs.at[SEG, src], xs.at[SEG, src], ag_r.at[SEG - 1, d - 1]).wait()
    for g in range(SEG):
        out_ref[0, :, g * PIECE : (g + 1) * PIECE] = xs[c + 1, g]

    for d in range(1, SEG):
        stage(d).wait_send()
        gain_copy(d).wait_send()
        qkg_copy(d).wait_send()

    @pl.when(j != c)
    def _():
        stage(0).wait_send()

    for dj in range(GROUP):
        for dc in range(SEG):
            if dc or dj:
                stale_copy(dc, dj).wait_send()
    y_mate().wait_send()
    for dy in range(1, NY):
        for piece in range(2):
            y_copy(dy, piece).wait_send()
    for s in range(SEG):
        for way, hops in ((0, LONG), (1, SHORT)):
            for t in range(hops):
                ring(s, t, way).wait_send()
            for t in range(way, hops + 1):
                to_mate(s, t, way).wait_send()
        for d in range(1, SEG):
            rs_copy(s, d).wait_send()
            ag_copy(s, d).wait_send()


def per_device(x_in, stale_kv, owner, live, gain, qk_gain, w_qkv, w_out):
    vmem = pl.BlockSpec(memory_space=pltpu.VMEM)
    smem = pl.BlockSpec(memory_space=pltpu.SMEM)
    dma = pltpu.SemaphoreType.DMA
    return pl.pallas_call(
        kernel,
        out_shape=jax.ShapeDtypeStruct((1, ROWS, D), BF),
        in_specs=[vmem, vmem, smem, smem, vmem, vmem, vmem, vmem],
        out_specs=vmem,
        scratch_shapes=[
            pltpu.VMEM((SEG, SLOT, 2 * PIECE), BF),
            pltpu.VMEM((GROUP, SLOT, 2 * PIECE), BF),
            pltpu.VMEM((2, BLOCK, PIECE), BF),
            pltpu.VMEM((SEG, 2, NZ, NY // 2, BLOCK, PIECE), BF),
            pltpu.VMEM((SEG, ROWS, PIECE), BF),
            pltpu.VMEM((SEG, GROUP, ROWS, PIECE), BF),
            pltpu.VMEM((SEG, 1, D), F32),
            pltpu.VMEM((SEG, 2, HEAD), F32),
            pltpu.VMEM((SEG + 1, SEG, ROWS, PIECE), BF),
            pltpu.VMEM((SEG, SEG - 1, ROWS, PIECE), BF),
            pltpu.VMEM((SEG, SEG - 1, ROWS, PIECE), BF),
            pltpu.VMEM((ROWS, PIECE), F32),
            dma((SEG,)), dma((GROUP,)),
            dma((SEG - 1,)), dma((SEG - 1,)), dma((SEG - 1,)), dma((SEG - 1,)),
            dma((SEG * GROUP,)), dma((SEG,)),
            dma((2 * NY,)), dma((SEG,)),
            dma((SEG, LONG)), dma((SEG, LONG)), dma((SEG, SHORT)), dma((SEG, SHORT)),
            dma((SEG, NZ)), dma((SEG,)),
            dma((SEG, SEG - 1)), dma((SEG, SEG - 1)), dma((SEG, SEG - 1)), dma((SEG, SEG - 1)),
            dma((1,)),
        ],
        compiler_params=pltpu.CompilerParams(
            collective_id=0, has_side_effects=True, vmem_limit_bytes=40 * 2**20
        ),
    )(x_in, stale_kv[0], owner, live, gain, qk_gain[0], w_qkv[0], w_out[0].T)


def solution(mesh):
    in_specs = (
        P("patch", None),
        P("segment", "patch", None),
        P(),
        P("patch"),
        P("segment", None),
        P("segment", None, None),
        P("segment", "patch", None),
        P("segment", None, "patch"),
    )
    return jax.shard_map(
        per_device, mesh=mesh, in_specs=in_specs, out_specs=P("segment", "patch", None), check_vma=False
    )
```

time: 366 us -> 125 us (0.34)
  the two profiles are of different devices: /device:TPU:14 before, /device:TPU:1 now
where the time goes in v1:
time: 125 us
  Pallas kernels  120 us (96%)
  local copies, waits for them, and re-layouts  4.21 us (3%)
    pallas_call x1, Pallas kernels, per_device(): pl.pallas_call(kernel, out_shape=jax.ShapeDtypeStruct((1, ROWS, D), BF),...  120 us
    unnamed x14, local copies, waits for them, and re-layouts  4.21 us

profile of v1, /device:TPU:1, one launch (start us, length us, event | category | flops | bytes accessed | tf_op | source)
XLA Modules:
  0.0 125.1 jit_solution(10474999615357956907)
XLA Ops:
  0.0 0.0 copy-start.3
  0.7 0.0 copy-start.4
  0.7 0.0 copy-start.5
  0.7 0.8 copy.9.owner_ref
  1.5 0.0 copy-done.3
  1.5 0.0 copy-done.4
  1.5 0.0 copy-done.5
  1.5 0.0 copy-start
  1.5 0.9 copy-done
  2.4 0.0 copy-start.1
  2.4 0.9 copy-done.1
  3.3 0.0 copy-start.2
  3.3 0.9 copy-done.2
  4.2 120.2 %shard_map.82 = bf16[1,64,1536]{2,1,0:T(8,128)(2,1)S(1)} custom-call(bf16[64,1536]{1,0:T(8,128)(2,1)S(1)} %copy-done, bf16[64,1536]{1,0:T(8,128)(2,1)S(1)} %bitcast.6, s32[32,16]{1,0:T(8,128)S(1)} %copy.9.owner_ref, s32[1]{0:T(128)S(6)} %copy.11.live_ref, f32[1,1536]{1,0:T(1,128)S(1)} %copy-done.4, f32[2,64]{1,0:T(2,128)S(1)} %bitcast.9, ...), custom_call_target="tpu_custom_call" | custom-call | tf_op jit(solution)/shard_map/pallas_call | solution.py:377
  124.4 0.7 copy.12
Async XLA Ops:
  0.0 1.5 %copy-start.3 = (bf16[1,768,12]{1,2,0:T(8,128)(2,1)S(1)}, bf16[1,768,12]{1,2,0:T(8,128)(2,1)}, u32[]{:S(2)}) copy-start(bf16[1,768,12]{1,2,0:T(8,128)(2,1)} %param.15) | copy-start | bytes 55300
  0.7 0.8 copy-start.4
  0.7 0.8 copy-start.5
  1.5 0.9 copy-start
  2.4 0.9 copy-start.1
  3.3 0.9 copy-start.2

commit v2 on v1

--- a/solution.py
+++ b/solution.py
@@ -33,11 +33,12 @@
 
 
 def kernel(
-    x_ref, stale_ref, owner_ref, live_ref, gain_ref, qkg_ref, wqkv_ref, wout_ref,
+    x_hbm, stale_hbm, owner_ref, live_ref, gain_hbm, qkg_hbm, wqkv_hbm, wout_hbm,
     out_ref,
+    x_ref, stale_ref, gain_ref, qkg_ref, wqkv_ref, wout_ref,
     wsend, stg, blk, w, stsend, st, gains, qkgs, xs, rs_out, rs_in, own_part,
-    wst_s, wst_r, g_s, g_r, qg_s, qg_r, st_s, st_r, y_s, y_r,
-    rl_s, rl_r, sh_s, sh_r, m_s, m_r, rs_s, rs_r, ag_s, ag_r, loc,
+    in_sem, wst_s, wst_r, g_s, g_r, qg_s, qg_r, st_s, st_r, y_s, y_r,
+    rl_s, rl_r, sh_s, sh_r, m_s, m_r, rs_s, rs_r, ag_s, ag_r,
 ):
     c = lax.axis_index("segment")
     p = lax.axis_index("patch")
@@ -47,6 +48,7 @@
     y = (p // 2) % NY
     z = p // (2 * NY)
     yp = y // 2
+    zh = z // 4
     mate = p + 1 - 2 * core
 
     def dev(seg, patch):
@@ -54,6 +56,18 @@
 
     def patch_of(zz, yy, cc):
         return zz * (2 * NY) + yy * 2 + cc
+
+    inputs = [
+        pltpu.make_async_copy(src, dst, in_sem.at[n])
+        for n, (src, dst) in enumerate(
+            [
+                (wqkv_hbm, wqkv_ref), (wout_hbm, wout_ref), (stale_hbm, stale_ref),
+                (gain_hbm, gain_ref), (qkg_hbm, qkg_ref), (x_hbm, x_ref),
+            ]
+        )
+    ]
+    for copy in inputs:
+        copy.start()
 
     barrier = pltpu.get_barrier_semaphore()
     partners = []
@@ -65,29 +79,21 @@
         pair = (yp + dy) % (NY // 2)
         for low in range(4):
             partners.append(dev(c, z * (2 * NY) + pair * 4 + low))
-    step = 1 - 2 * core
-    z_long = (z + step + NZ) % NZ
-    z_short = (z - step + NZ) % NZ
-    partners.append(dev(c, patch_of(z_long, y, core)))
-    partners.append(dev(c, patch_of(z_short, y, core)))
+    for dz in range(1, NZ):
+        for low in range(2):
+            partners.append(dev(c, patch_of((z + dz) % NZ, y, low)))
     for partner in partners:
         pl.semaphore_signal(barrier, inc=1, device_id=partner, device_id_type=MESH)
 
     wsend[...] = jnp.zeros_like(wsend)
+    inputs[0].wait()
+    inputs[1].wait()
     for g in range(SEG):
         for part in range(3):
-            wsend[g, 0:SHARD, part * GW : (part + 1) * GW] = wqkv_ref[
+            wsend[part // 2, g, 0:SHARD, part % 2 * GW : (part % 2 + 1) * GW] = wqkv_ref[
                 :, part * HD + g * GW : part * HD + (g + 1) * GW
             ]
-        wsend[g, 0:SHARD, 3 * GW :] = wout_ref[:, g * GW : (g + 1) * GW]
-        for part in range(2):
-            stsend[g, :, part * GW : (part + 1) * GW] = stale_ref[
-                :, part * HD + g * GW : part * HD + (g + 1) * GW
-            ]
-    for g in range(SEG):
-        xs[0, g] = x_ref[:, g * PIECE : (g + 1) * PIECE]
-    gains[c] = gain_ref[...]
-    qkgs[c] = qkg_ref[...]
+        wsend[1, g, 0:SHARD, GW:] = wout_ref[:, g * GW : (g + 1) * GW]
     pl.semaphore_wait(barrier, len(partners))
 
     def remote(src, dst, ss, rs, device):
@@ -96,35 +102,40 @@
             device_id=device, device_id_type=MESH,
         )
 
-    def stage(d):
+    holder = [2 * (1 - zh) + c % 2, 2 * zh + c % 2]
+    holds_a = y % 2 != zh
+
+    def stage(d, piece):
         g = (c + d) % SEG
         return remote(
-            wsend.at[g], stg.at[j], wst_s.at[d], wst_r.at[j], dev(g, image * GROUP + c)
-        )
-
-    def stage_local():
-        return pltpu.make_async_copy(wsend.at[c], stg.at[j], wst_r.at[j])
-
-    for d in range(1, SEG):
-        stage(d).start()
-
-    @pl.when(j == c)
-    def _():
-        stage_local().start()
-
-    @pl.when(j != c)
-    def _():
-        stage(0).start()
+            wsend.at[piece, g], stg.at[c // 2, j], wst_s.at[d, piece], wst_r.at[c // 2],
+            dev(g, image * GROUP + holder[piece]),
+        )
+
+    for d in range(SEG):
+        for piece in range(2):
+            if d:
+                stage(d, piece).start()
+                continue
+
+            @pl.when(j == holder[piece])
+            def _():
+                pltpu.make_async_copy(wsend.at[piece, c], stg.at[c // 2, j], wst_r.at[c // 2]).start()
+
+            @pl.when(j != holder[piece])
+            def _():
+                stage(0, piece).start()
+
+    inputs[3].wait()
+    inputs[4].wait()
+    gains[c] = gain_ref[...]
+    qkgs[c] = qkg_ref[...]
 
     def gain_copy(d):
         return remote(gain_ref, gains.at[c], g_s.at[d - 1], g_r.at[d - 1], dev((c + d) % SEG, p))
 
     def qkg_copy(d):
         return remote(qkg_ref, qkgs.at[c], qg_s.at[d - 1], qg_r.at[d - 1], dev((c + d) % SEG, p))
-
-    for d in range(1, SEG):
-        gain_copy(d).start()
-        qkg_copy(d).start()
 
     def stale_copy(dc, dj):
         g = (c + dc) % SEG
@@ -133,68 +144,80 @@
             dev(g, image * GROUP + (j + dj) % GROUP),
         )
 
-    pltpu.make_async_copy(stsend.at[c], st.at[c, j], st_r.at[c]).start()
-    for dj in range(GROUP):
-        for dc in range(SEG):
-            if dc or dj:
-                stale_copy(dc, dj).start()
-
-    for slot in range(GROUP):
-        pltpu.make_async_copy(wsend.at[0], stg.at[slot], wst_r.at[slot]).wait()
     a = lax.broadcasted_iota(jnp.int32, (BLOCK, GROUP * SLOT), 0)
     b = lax.broadcasted_iota(jnp.int32, (BLOCK, GROUP * SLOT), 1)
     pick = jnp.zeros((BLOCK, GROUP * SLOT), F32)
     for slot in range(GROUP):
         hit = (a - SHARD * slot == b - SLOT * slot) & (b >= SLOT * slot) & (b < SLOT * slot + SHARD)
         pick = jnp.where(hit, 1.0, pick)
-    packed = jnp.dot(
-        pick.astype(BF), stg[...].reshape(GROUP * SLOT, 2 * PIECE), preferred_element_type=F32
-    ).astype(BF)
-    blk[0] = packed[:, :PIECE]
-    blk[1] = packed[:, PIECE:]
-
-    def y_copy(dy, piece):
-        target = patch_of(z, (y + dy) % NY, piece)
-        return remote(
-            blk.at[piece], w.at[j, piece, z, yp], y_s.at[dy * 2 + piece], y_r.at[j], dev(c, target)
-        )
-
-    def y_mate():
-        return remote(
-            blk.at[1 - core], w.at[j, 1 - core, z, yp], y_s.at[0], y_r.at[j], dev(c, mate)
-        )
-
-    def y_start(s):
-        @pl.when(j == s)
+    pick = pick.astype(BF)
+
+    def compact(half):
+        pltpu.make_async_copy(stg.at[half], stg.at[half], wst_r.at[half]).wait()
+        blk[half] = jnp.dot(
+            pick, stg[half].reshape(GROUP * SLOT, PIECE), preferred_element_type=F32
+        ).astype(BF)
+
+    def spread(half, piece, delta):
+        s = core + 2 * half
+        if piece == 0:
+            target = patch_of(z, (y + delta) % NY, 0)
+            dst = w.at[s, 0, z, yp]
+        else:
+            target = patch_of((z + delta) % NZ, y, 1)
+            dst = w.at[s, 1, y, z % 4]
+        return remote(blk.at[half], dst, y_s.at[half, delta], y_r.at[s], dev(c, target))
+
+    def spread_all(half, act):
+        for piece in range(2):
+
+            @pl.when(holds_a if piece == 0 else jnp.logical_not(holds_a))
+            def _():
+                @pl.when(core != piece)
+                def _():
+                    act(spread(half, piece, 0))
+
+                for delta in (1, 7, 2, 6, 3, 5, 4):
+                    act(spread(half, piece, delta))
+
+    def spread_start(half):
+        s = core + 2 * half
+
+        @pl.when(jnp.logical_and(holds_a, core == 0))
         def _():
-            pltpu.make_async_copy(blk.at[core], w.at[j, core, z, yp], y_r.at[j]).start()
-            y_mate().start()
-            for dy in (1, 7, 2, 6, 3, 5, 4):
-                for piece in range(2):
-                    y_copy(dy, piece).start()
+            pltpu.make_async_copy(blk.at[half], w.at[s, 0, z, yp], y_r.at[s]).start()
+
+        @pl.when(jnp.logical_and(jnp.logical_not(holds_a), core == 1))
+        def _():
+            pltpu.make_async_copy(blk.at[half], w.at[s, 1, y, z % 4], y_r.at[s]).start()
+
+        spread_all(half, lambda copy: copy.start())
+
+    place = jnp.where(core == 0, z, y)
+
+    def neighbour(step):
+        nz = jnp.where(core == 0, (z + step + NZ) % NZ, z)
+        ny = jnp.where(core == 0, y, (y + step + NY) % NY)
+        return dev(c, patch_of(nz, ny, core))
+
+    up, down = neighbour(1), neighbour(-1)
+
+    def ring_block(s, t, way):
+        step = 1 if (s + way) % 2 == 0 else -1
+        return w.at[s, core, (place - step * t + NZ) % NZ]
 
     def ring(s, t, way):
-        if way == 0:
-            source, target, ss, rs = z - step * t, z_long, rl_s, rl_r
-        else:
-            source, target, ss, rs = z + step * t, z_short, sh_s, sh_r
-        block = w.at[s, core, (source + NZ) % NZ]
-        return remote(block, block, ss.at[s, t], rs.at[s, t], dev(c, patch_of(target, y, core)))
+        ss, rs = (rl_s, rl_r) if way == 0 else (sh_s, sh_r)
+        block = ring_block(s, t, way)
+        return remote(block, block, ss.at[s, t], rs.at[s, t], up if (s + way) % 2 == 0 else down)
 
     def to_mate(s, t, way):
-        source = z - step * t if way == 0 else z + step * t
-        block = w.at[s, core, (source + NZ) % NZ]
+        block = ring_block(s, t, way)
         index = t if way == 0 else LONG + t
         return remote(block, block, m_s.at[s, index], m_r.at[s], dev(c, mate))
 
-    def ring_wait(s, t, way):
-        source = z - step * t if way == 0 else z + step * t
-        block = w.at[s, core, (source + NZ) % NZ]
-        rs = rl_r if way == 0 else sh_r
-        pltpu.make_async_copy(block, block, rs.at[s, t - 1]).wait()
-
     def ring_start(s):
-        block = w.at[s, core, z]
+        block = w.at[s, core, place]
         pltpu.make_async_copy(block, block, y_r.at[s]).wait()
         ring(s, 0, 0).start()
         ring(s, 0, 1).start()
@@ -203,21 +226,45 @@
     def ring_round(s, t):
         for way, hops in ((0, LONG), (1, SHORT)):
             if t <= hops:
-                ring_wait(s, t, way)
+                block = ring_block(s, t, way)
+                rs = rl_r if way == 0 else sh_r
+                pltpu.make_async_copy(block, block, rs.at[s, t - 1]).wait()
                 if t < hops:
                     ring(s, t, way).start()
                 to_mate(s, t, way).start()
 
-    y_start(0)
-    ring_start(0)
-    y_start(1)
-    ring_round(0, 1)
-    y_start(2)
-    ring_round(0, 2)
-    y_start(3)
-    ring_round(0, 3)
-    ring_start(1)
-    ring_round(0, 4)
+    def serve(plan):
+        for s, t in plan:
+            if t == 0:
+                ring_start(s)
+            else:
+                ring_round(s, t)
+
+    compact(0)
+    spread_start(0)
+    for d in range(1, SEG):
+        gain_copy(d).start()
+        qkg_copy(d).start()
+    compact(1)
+
+    inputs[2].wait()
+    for g in range(SEG):
+        for part in range(2):
+            stsend[g, :, part * GW : (part + 1) * GW] = stale_ref[
+                :, part * HD + g * GW : part * HD + (g + 1) * GW
+            ]
+    pltpu.make_async_copy(stsend.at[c], st.at[c, j], st_r.at[c]).start()
+    for dj in range(GROUP):
+        for dc in range(SEG):
+            if dc or dj:
+                stale_copy(dc, dj).start()
+    inputs[5].wait()
+    for g in range(SEG):
+        xs[0, g] = x_ref[:, g * PIECE : (g + 1) * PIECE]
+
+    serve([(0, 0)])
+    spread_start(1)
+    serve([(0, 1), (1, 0), (0, 2), (1, 1), (0, 3), (1, 2), (0, 4)])
 
     lane_g = lax.broadcasted_iota(jnp.int32, (1, GW), 1)
     head_of = [(lane_g >= h * HEAD) & (lane_g < (h + 1) * HEAD) for h in range(GH)]
@@ -228,7 +275,7 @@
     barred = jnp.zeros((ROWS, IMG), jnp.int32)
     live_count = live_ref[0]
     for m in range(MICRO):
-        first = owner_ref[image, j * MICRO + m] * MROWS
+        first = owner_ref[j * MICRO + m, image] * MROWS
         hit = (row >= m * MROWS) & (row < (m + 1) * MROWS) & (key_row >= first) & (key_row < first + MROWS)
         barred = jnp.where(hit, 1, barred)
     far_mask = jnp.where(barred == 1, 0.0, 1.0)
@@ -271,7 +318,10 @@
         inverse = lax.rsqrt(jnp.mean(x * x, -1, keepdims=True) + 1e-06)
         normed = (x * inverse * gains[s]).astype(BF)
         qk = jnp.dot(normed, w[s, 0].reshape(D, PIECE), preferred_element_type=F32).astype(BF).astype(F32)
-        value = jnp.dot(normed, w[s, 1].reshape(D, PIECE), preferred_element_type=F32).astype(BF)
+        w_b = jnp.concatenate(
+            [w[s, 1, 2 * b + zz // 4, zz % 4] for zz in range(NZ) for b in range(NY // 2)], 0
+        )
+        value = jnp.dot(normed, w_b, preferred_element_type=F32).astype(BF)
         gq = qkgs[s, 0:1, :]
         gk = qkgs[s, 1:2, :]
         query = head_norm(qk[:, :GW], jnp.concatenate([gq] * GH, 1))
@@ -294,7 +344,14 @@
         attended = attended.astype(BF)
         for d in (1, 2, 3, 0):
             g = (c + d) % SEG
-            rows = w[s, 1, pl.ds(2 * g, 2), :, :, PIECE - 256 :].reshape(PIECE, 256)
+            rows = jnp.concatenate(
+                [
+                    w[s, 1, 2 * b + g // 2, 2 * (g % 2) + zz, :, PIECE - 256 :]
+                    for zz in range(2)
+                    for b in range(NY // 2)
+                ],
+                0,
+            )
             part = nt(attended, rows)
             if d:
                 rs_out[s, d - 1] = part.astype(BF)
@@ -324,17 +381,13 @@
         for d in range(1, SEG):
             ag_copy(s, d).start()
 
+    middle = [[(1, 3), (2, 0)], [(2, 3), (3, 1)], [(3, 3)], []]
+    after = [[(1, 4), (2, 1), (3, 0), (2, 2)], [(2, 4), (3, 2)], [(3, 4)], []]
     for s in range(SEG):
         chain_front(s)
-        if s + 1 < SEG:
-            ring_round(s + 1, 1)
+        serve(middle[s])
         chain_back(s)
-        if s + 1 < SEG:
-            ring_round(s + 1, 2)
-            ring_round(s + 1, 3)
-            if s + 2 < SEG:
-                ring_start(s + 2)
-            ring_round(s + 1, 4)
+        serve(after[s])
 
     for d in range(1, SEG):
         src = (c + SEG - d) % SEG
@@ -342,23 +395,25 @@
     for g in range(SEG):
         out_ref[0, :, g * PIECE : (g + 1) * PIECE] = xs[c + 1, g]
 
+    for d in range(SEG):
+        for piece in range(2):
+            if d:
+                stage(d, piece).wait_send()
+            else:
+
+                @pl.when(j != holder[piece])
+                def _():
+                    stage(0, piece).wait_send()
+
     for d in range(1, SEG):
-        stage(d).wait_send()
         gain_copy(d).wait_send()
         qkg_copy(d).wait_send()
-
-    @pl.when(j != c)
-    def _():
-        stage(0).wait_send()
-
     for dj in range(GROUP):
         for dc in range(SEG):
             if dc or dj:
                 stale_copy(dc, dj).wait_send()
-    y_mate().wait_send()
-    for dy in range(1, NY):
-        for piece in range(2):
-            y_copy(dy, piece).wait_send()
+    for half in range(2):
+        spread_all(half, lambda copy: copy.wait_send())
     for s in range(SEG):
         for way, hops in ((0, LONG), (1, SHORT)):
             for t in range(hops):
@@ -372,16 +427,23 @@
 
 def per_device(x_in, stale_kv, owner, live, gain, qk_gain, w_qkv, w_out):
     vmem = pl.BlockSpec(memory_space=pltpu.VMEM)
+    hbm = pl.BlockSpec(memory_space=pltpu.HBM)
     smem = pl.BlockSpec(memory_space=pltpu.SMEM)
     dma = pltpu.SemaphoreType.DMA
     return pl.pallas_call(
         kernel,
         out_shape=jax.ShapeDtypeStruct((1, ROWS, D), BF),
-        in_specs=[vmem, vmem, smem, smem, vmem, vmem, vmem, vmem],
+        in_specs=[hbm, hbm, smem, smem, hbm, hbm, hbm, hbm],
         out_specs=vmem,
         scratch_shapes=[
-            pltpu.VMEM((SEG, SLOT, 2 * PIECE), BF),
-            pltpu.VMEM((GROUP, SLOT, 2 * PIECE), BF),
+            pltpu.VMEM((ROWS, D), BF),
+            pltpu.VMEM((ROWS, D), BF),
+            pltpu.VMEM((1, D), F32),
+            pltpu.VMEM((2, HEAD), F32),
+            pltpu.VMEM((SHARD, 3 * HD), BF),
+            pltpu.VMEM((SHARD, HD), BF),
+            pltpu.VMEM((2, SEG, SLOT, PIECE), BF),
+            pltpu.VMEM((2, GROUP, SLOT, PIECE), BF),
             pltpu.VMEM((2, BLOCK, PIECE), BF),
             pltpu.VMEM((SEG, 2, NZ, NY // 2, BLOCK, PIECE), BF),
             pltpu.VMEM((SEG, ROWS, PIECE), BF),
@@ -392,19 +454,18 @@
             pltpu.VMEM((SEG, SEG - 1, ROWS, PIECE), BF),
             pltpu.VMEM((SEG, SEG - 1, ROWS, PIECE), BF),
             pltpu.VMEM((ROWS, PIECE), F32),
-            dma((SEG,)), dma((GROUP,)),
+            dma((6,)), dma((SEG, 2)), dma((2,)),
             dma((SEG - 1,)), dma((SEG - 1,)), dma((SEG - 1,)), dma((SEG - 1,)),
             dma((SEG * GROUP,)), dma((SEG,)),
-            dma((2 * NY,)), dma((SEG,)),
+            dma((2, NY)), dma((SEG,)),
             dma((SEG, LONG)), dma((SEG, LONG)), dma((SEG, SHORT)), dma((SEG, SHORT)),
             dma((SEG, NZ)), dma((SEG,)),
             dma((SEG, SEG - 1)), dma((SEG, SEG - 1)), dma((SEG, SEG - 1)), dma((SEG, SEG - 1)),
-            dma((1,)),
         ],
         compiler_params=pltpu.CompilerParams(
-            collective_id=0, has_side_effects=True, vmem_limit_bytes=40 * 2**20
+            collective_id=0, has_side_effects=True, vmem_limit_bytes=62 * 2**20
         ),
-    )(x_in, stale_kv[0], owner, live, gain, qk_gain[0], w_qkv[0], w_out[0].T)
+    )(x_in, stale_kv[0], owner.T, live, gain, qk_gain[0], w_qkv[0], w_out[0].T)
 
 
 def solution(mesh):

time: 125 us -> 97.3 us (0.78)
  the two profiles are of different devices: /device:TPU:1 before, /device:TPU:6 now
where the time goes in v2:
time: 97.3 us; the launch traced here: 95.3 us
  Pallas kernels  93.1 us (96%)
  local copies, waits for them, and re-layouts  1.62 us (2%)
    pallas_call x1, Pallas kernels, per_device(): pl.pallas_call(kernel, out_shape=jax.ShapeDtypeStruct((1, ROWS, D), BF),...  93.1 us

profile of v2, /device:TPU:6, one launch (start us, length us, event | category | flops | bytes accessed | tf_op | source)
XLA Modules:
  0.0 95.3 jit_solution(6421934903761148675)
XLA Ops:
  0.7 93.1 %shard_map.82 = bf16[1,64,1536]{2,1,0:T(8,128)(2,1)} custom-call(bf16[64,1536]{1,0:T(8,128)(2,1)} %x_hbm.1, bf16[64,1536]{1,0:T(8,128)(2,1)} %bitcast.7, s32[16,32]{1,0:T(8,128)} %bitcast.10, s32[1]{0:T(128)S(6)} %copy.10.live_ref, f32[1,1536]{1,0:T(1,128)} %gain_hbm.1, f32[2,64]{1,0:T(2,128)} %bitcast.11, bf16[12,2304]{1,0:T(8,128)(2,1)} %bitcast.8, ...), custom_call_target="tpu_custom_call" | custom-call | tf_op jit(solution)/shard_map/pallas_call | solution.py:433
  93.7 1.6 %copy.11 = bf16[1,64,1536]{2,1,0:T(8,128)(2,1)} copy(bf16[1,64,1536]{2,1,0:T(8,128)(2,1)} %shard_map.82) | data formatting | bytes 393216

commit v3 on v2

--- a/solution.py
+++ b/solution.py
@@ -29,7 +29,10 @@
 D = 1536
 HD = 768
 LONG = NZ // 2
-SHORT = NZ - 1 - LONG
+PARTS = (2, 1, 1, 1)
+BEFORE = [(0, 0), (1, -1), (-1, 0), (0, 1), (0, 2), (1, 0), (2, -1), (0, 3), (-1, 1), (1, 1)]
+MIDDLE = [[(2, 0), (3, -1), (1, 2)], [(3, 0), (2, 2)], [(3, 2)], []]
+AFTER = [[(1, 3), (2, 1)], [(2, 3), (3, 1)], [(3, 3)], []]
 
 
 def kernel(
@@ -38,7 +41,7 @@
     x_ref, stale_ref, gain_ref, qkg_ref, wqkv_ref, wout_ref,
     wsend, stg, blk, w, stsend, st, gains, qkgs, xs, rs_out, rs_in, own_part,
     in_sem, wst_s, wst_r, g_s, g_r, qg_s, qg_r, st_s, st_r, y_s, y_r,
-    rl_s, rl_r, sh_s, sh_r, m_s, m_r, rs_s, rs_r, ag_s, ag_r,
+    ring_s, ring_r, m_s, m_r, rs_s, rs_r, ag_s, ag_r,
 ):
     c = lax.axis_index("segment")
     p = lax.axis_index("patch")
@@ -128,21 +131,35 @@
 
     inputs[3].wait()
     inputs[4].wait()
-    gains[c] = gain_ref[...]
+    for g in range(SEG):
+        gains[c, g] = gain_ref[:, g * PIECE : (g + 1) * PIECE]
     qkgs[c] = qkg_ref[...]
 
     def gain_copy(d):
-        return remote(gain_ref, gains.at[c], g_s.at[d - 1], g_r.at[d - 1], dev((c + d) % SEG, p))
+        return remote(gains.at[c], gains.at[c], g_s.at[d - 1], g_r.at[d - 1], dev((c + d) % SEG, p))
 
     def qkg_copy(d):
         return remote(qkg_ref, qkgs.at[c], qg_s.at[d - 1], qg_r.at[d - 1], dev((c + d) % SEG, p))
 
-    def stale_copy(dc, dj):
-        g = (c + dc) % SEG
-        return remote(
-            stsend.at[g], st.at[c, j], st_s.at[dc * GROUP + dj], st_r.at[c],
-            dev(g, image * GROUP + (j + dj) % GROUP),
-        )
+    across = p + 2 - 4 * (y % 2)
+    j_across = (j + 2) % GROUP
+
+    def stale_copy(d):
+        g = (c + d) % SEG
+        return remote(stsend.at[g], st.at[c, j], st_s.at[d], st_r.at[0], dev(g, p))
+
+    def stale_across():
+        return remote(st.at[:, j], st.at[:, j], st_s.at[0], st_r.at[1], dev(c, across))
+
+    def stale_mate():
+        return remote(st.at[:, j], st.at[:, j], st_s.at[4], st_r.at[2], dev(c, mate))
+
+    def stale_mate_across():
+        return remote(st.at[:, j_across], st.at[:, j_across], st_s.at[5], st_r.at[3], dev(c, mate))
+
+    def stale_wait(n, index):
+        block = st.at[:, index]
+        pltpu.make_async_copy(block, block, st_r.at[n]).wait()
 
     a = lax.broadcasted_iota(jnp.int32, (BLOCK, GROUP * SLOT), 0)
     b = lax.broadcasted_iota(jnp.int32, (BLOCK, GROUP * SLOT), 1)
@@ -162,36 +179,38 @@
         s = core + 2 * half
         if piece == 0:
             target = patch_of(z, (y + delta) % NY, 0)
-            dst = w.at[s, 0, z, yp]
+            dst, slot = w.at[s, 0, z, yp], yp
         else:
             target = patch_of((z + delta) % NZ, y, 1)
-            dst = w.at[s, 1, y, z % 4]
-        return remote(blk.at[half], dst, y_s.at[half, delta], y_r.at[s], dev(c, target))
-
-    def spread_all(half, act):
+            dst, slot = w.at[s, 1, y, z % 4], z % 4
+        return remote(blk.at[half], dst, y_s.at[half, delta], y_r.at[s, slot], dev(c, target))
+
+    def spread_all(s, act):
+        half = s // 2
         for piece in range(2):
 
-            @pl.when(holds_a if piece == 0 else jnp.logical_not(holds_a))
+            @pl.when((core == s % 2) & (holds_a if piece == 0 else jnp.logical_not(holds_a)))
             def _():
-                @pl.when(core != piece)
-                def _():
+                if s % 2 != piece:
                     act(spread(half, piece, 0))
-
                 for delta in (1, 7, 2, 6, 3, 5, 4):
                     act(spread(half, piece, delta))
 
-    def spread_start(half):
-        s = core + 2 * half
-
-        @pl.when(jnp.logical_and(holds_a, core == 0))
-        def _():
-            pltpu.make_async_copy(blk.at[half], w.at[s, 0, z, yp], y_r.at[s]).start()
-
-        @pl.when(jnp.logical_and(jnp.logical_not(holds_a), core == 1))
-        def _():
-            pltpu.make_async_copy(blk.at[half], w.at[s, 1, y, z % 4], y_r.at[s]).start()
-
-        spread_all(half, lambda copy: copy.start())
+    def spread_start(s):
+        half = s // 2
+        if s % 2 == 0:
+
+            @pl.when((core == 0) & holds_a)
+            def _():
+                pltpu.make_async_copy(blk.at[half], w.at[s, 0, z, yp], y_r.at[s, yp]).start()
+
+        else:
+
+            @pl.when((core == 1) & jnp.logical_not(holds_a))
+            def _():
+                pltpu.make_async_copy(blk.at[half], w.at[s, 1, y, z % 4], y_r.at[s, z % 4]).start()
+
+        spread_all(s, lambda copy: copy.start())
 
     place = jnp.where(core == 0, z, y)
 
@@ -200,48 +219,89 @@
         ny = jnp.where(core == 0, y, (y + step + NY) % NY)
         return dev(c, patch_of(nz, ny, core))
 
-    up, down = neighbour(1), neighbour(-1)
-
-    def ring_block(s, t, way):
-        step = 1 if (s + way) % 2 == 0 else -1
-        return w.at[s, core, (place - step * t + NZ) % NZ]
-
-    def ring(s, t, way):
-        ss, rs = (rl_s, rl_r) if way == 0 else (sh_s, sh_r)
-        block = ring_block(s, t, way)
-        return remote(block, block, ss.at[s, t], rs.at[s, t], up if (s + way) % 2 == 0 else down)
-
-    def to_mate(s, t, way):
-        block = ring_block(s, t, way)
-        index = t if way == 0 else LONG + t
-        return remote(block, block, m_s.at[s, index], m_r.at[s], dev(c, mate))
+    near = jnp.where(core == 0, yp, z % 4)
+
+    def ring_block(s, way, distance, q):
+        size = GROUP // PARTS[s]
+        source = (place - (1 - 2 * way) * distance + NZ) % NZ
+        part = (near // size + q) % PARTS[s]
+        return w.at[s, core, source, pl.ds(part * size, size)], part
+
+    def arrival_index(s, way, distance, part):
+        n = 2 * (distance - 1) + (way if distance < LONG else 0)
+        return (NZ - 1) * sum(PARTS[:s]) + n * PARTS[s] + part
+
+    def ring_copy(s, way, held, step, q):
+        block, part = ring_block(s, way, held, q)
+        arrival = ring_r.at[arrival_index(s, way, held + step, part)]
+        return remote(block, block, ring_s.at[s], arrival, neighbour((1 - 2 * way) * step))
+
+    def ring_wait(s, way, distance, q):
+        block, part = ring_block(s, way, distance, q)
+        pltpu.make_async_copy(block, block, ring_r.at[arrival_index(s, way, distance, part)]).wait()
+
+    def to_mate(s, way, distance, q):
+        block, _ = ring_block(s, way, distance, q)
+        return remote(block, block, m_s.at[s], m_r.at[s], dev(c, mate))
+
+    def arrivals(s):
+        return [(way, distance) for distance in range(1, LONG + 1) for way in range(2) if distance < LONG or way == s % 2]
 
     def ring_start(s):
-        block = w.at[s, core, place]
-        pltpu.make_async_copy(block, block, y_r.at[s]).wait()
-        ring(s, 0, 0).start()
-        ring(s, 0, 1).start()
-        to_mate(s, 0, 0).start()
-
-    def ring_round(s, t):
-        for way, hops in ((0, LONG), (1, SHORT)):
-            if t <= hops:
-                block = ring_block(s, t, way)
-                rs = rl_r if way == 0 else sh_r
-                pltpu.make_async_copy(block, block, rs.at[s, t - 1]).wait()
-                if t < hops:
-                    ring(s, t, way).start()
-                to_mate(s, t, way).start()
+        for q in range(PARTS[s]):
+            block, part = ring_block(s, 0, 0, q)
+            size = GROUP // PARTS[s]
+            for n in range(size):
+                one = w.at[s, core, place, part * size + n]
+                pltpu.make_async_copy(one, one, y_r.at[s, part * size + n]).wait()
+            for step in (2, 1):
+                for way in range(2):
+                    ring_copy(s, way, 0, step, q).start()
+        for q in range(PARTS[s]):
+            to_mate(s, 0, 0, q).start()
+
+    def ring_forward(s):
+        for q in range(PARTS[s]):
+            for way in range(2):
+                ring_wait(s, way, 2, q)
+                ring_copy(s, way, 2, 1, q).start()
+                if way == s % 2:
+                    ring_copy(s, way, 2, 2, q).start()
+        for q in range(PARTS[s]):
+            for way in range(2):
+                to_mate(s, way, 2, q).start()
+
+    def ring_hand(s, distances):
+        for way, distance in arrivals(s):
+            if distance in distances:
+                for q in range(PARTS[s]):
+                    ring_wait(s, way, distance, q)
+                    to_mate(s, way, distance, q).start()
+
+    def stale_step(n):
+        if n == 0:
+            stale_wait(0, j)
+            stale_across().start()
+            stale_mate().start()
+        else:
+            stale_wait(1, j_across)
+            stale_mate_across().start()
 
     def serve(plan):
         for s, t in plan:
-            if t == 0:
+            if s < 0:
+                stale_step(t)
+            elif t < 0:
+                spread_start(s)
+            elif t == 0:
                 ring_start(s)
+            elif t == 1:
+                ring_forward(s)
             else:
-                ring_round(s, t)
+                ring_hand(s, (1,) if t == 2 else (3, 4))
 
     compact(0)
-    spread_start(0)
+    serve([(0, -1)])
     for d in range(1, SEG):
         gain_copy(d).start()
         qkg_copy(d).start()
@@ -253,18 +313,14 @@
             stsend[g, :, part * GW : (part + 1) * GW] = stale_ref[
                 :, part * HD + g * GW : part * HD + (g + 1) * GW
             ]
-    pltpu.make_async_copy(stsend.at[c], st.at[c, j], st_r.at[c]).start()
-    for dj in range(GROUP):
-        for dc in range(SEG):
-            if dc or dj:
-                stale_copy(dc, dj).start()
+    pltpu.make_async_copy(stsend.at[c], st.at[c, j], st_r.at[0]).start()
+    for d in range(1, SEG):
+        stale_copy(d).start()
     inputs[5].wait()
     for g in range(SEG):
         xs[0, g] = x_ref[:, g * PIECE : (g + 1) * PIECE]
 
-    serve([(0, 0)])
-    spread_start(1)
-    serve([(0, 1), (1, 0), (0, 2), (1, 1), (0, 3), (1, 2), (0, 4)])
+    serve(BEFORE)
 
     lane_g = lax.broadcasted_iota(jnp.int32, (1, GW), 1)
     head_of = [(lane_g >= h * HEAD) & (lane_g < (h + 1) * HEAD) for h in range(GH)]
@@ -302,33 +358,44 @@
     def nt(lhs, rhs):
         return lax.dot_general(lhs, rhs, (((1,), (1,)), ((), ())), preferred_element_type=F32)
 
+    def w_b_rows(s, g):
+        return jnp.concatenate(
+            [w[s, 1, 2 * b + g // 2, 2 * (g % 2) + zz] for zz in range(2) for b in range(NY // 2)], 0
+        )
+
     def chain_front(s):
         other = 1 - core
         pltpu.make_async_copy(w.at[s, other], w.at[s, other], m_r.at[s]).wait()
         if s == 0:
             for d in range(1, SEG):
                 src = (c + SEG - d) % SEG
-                pltpu.make_async_copy(gain_ref, gains.at[src], g_r.at[d - 1]).wait()
+                pltpu.make_async_copy(gains.at[src], gains.at[src], g_r.at[d - 1]).wait()
                 pltpu.make_async_copy(qkg_ref, qkgs.at[src], qg_r.at[d - 1]).wait()
-        else:
-            for d in range(1, SEG):
-                src = (c + SEG - d) % SEG
-                pltpu.make_async_copy(xs.at[s, src], xs.at[s, src], ag_r.at[s - 1, d - 1]).wait()
-        x = jnp.concatenate([xs[s, g] for g in range(SEG)], 1).astype(F32)
-        inverse = lax.rsqrt(jnp.mean(x * x, -1, keepdims=True) + 1e-06)
-        normed = (x * inverse * gains[s]).astype(BF)
-        qk = jnp.dot(normed, w[s, 0].reshape(D, PIECE), preferred_element_type=F32).astype(BF).astype(F32)
-        w_b = jnp.concatenate(
-            [w[s, 1, 2 * b + zz // 4, zz % 4] for zz in range(NZ) for b in range(NY // 2)], 0
-        )
-        value = jnp.dot(normed, w_b, preferred_element_type=F32).astype(BF)
+        product_a = jnp.zeros((ROWS, PIECE), F32)
+        product_b = jnp.zeros((ROWS, PIECE), F32)
+        squares = jnp.zeros((ROWS, 1), F32)
+        for d in (0, 1, 3, 2):
+            g = (c + SEG - d) % SEG
+            if s and d:
+                pltpu.make_async_copy(xs.at[s, g], xs.at[s, g], ag_r.at[s - 1, d - 1]).wait()
+            x = xs[s, g].astype(F32)
+            squares = squares + jnp.sum(x * x, -1, keepdims=True)
+            scaled = (x * gains[s, g]).astype(BF)
+            w_a = w[s, 0, pl.ds(2 * g, 2)].reshape(PIECE, PIECE)
+            product_a = product_a + jnp.dot(scaled, w_a, preferred_element_type=F32)
+            product_b = product_b + jnp.dot(scaled, w_b_rows(s, g), preferred_element_type=F32)
+        inverse = lax.rsqrt(squares * (1.0 / D) + 1e-06)
+        qk = (product_a * inverse).astype(BF).astype(F32)
+        value = (product_b * inverse).astype(BF)
         gq = qkgs[s, 0:1, :]
         gk = qkgs[s, 1:2, :]
         query = head_norm(qk[:, :GW], jnp.concatenate([gq] * GH, 1))
         key = head_norm(qk[:, GW:], jnp.concatenate([gk] * GH, 1)).astype(BF)
         query = query.astype(BF).astype(F32)
         stacked = jnp.concatenate([jnp.where(head_of[h], query, 0.0) for h in range(GH)], 0).astype(BF)
-        pltpu.make_async_copy(st.at[s], st.at[s], st_r.at[s]).wait()
+        if s == 0:
+            stale_wait(2, j + 1 - 2 * core)
+            stale_wait(3, j_across + 1 - 2 * core)
         kv = st[s].reshape(IMG, PIECE)
         scale = HEAD**-0.5
         far = jnp.exp(nt(stacked, kv[:, :GW]) * scale) * far_mask
@@ -342,17 +409,9 @@
         for h in range(GH):
             attended = jnp.where(head_in_window[h], weighted[h * ROWS : (h + 1) * ROWS], attended)
         attended = attended.astype(BF)
-        for d in (1, 2, 3, 0):
+        for d in (2, 1, 3, 0):
             g = (c + d) % SEG
-            rows = jnp.concatenate(
-                [
-                    w[s, 1, 2 * b + g // 2, 2 * (g % 2) + zz, :, PIECE - 256 :]
-                    for zz in range(2)
-                    for b in range(NY // 2)
-                ],
-                0,
-            )
-            part = nt(attended, rows)
+            part = nt(attended, w_b_rows(s, g)[:, PIECE - 256 :])
             if d:
                 rs_out[s, d - 1] = part.astype(BF)
                 rs_copy(s, d).start()
@@ -361,19 +420,18 @@
 
     def rs_copy(s, d):
         return remote(
-            rs_out.at[s, d - 1], rs_in.at[s, d - 1], rs_s.at[s, d - 1], rs_r.at[s, d - 1],
+            rs_out.at[s, d - 1], rs_in.at[s, d - 1], rs_s.at[s], rs_r.at[s],
             dev((c + d) % SEG, p),
         )
 
     def ag_copy(s, d):
         return remote(
-            xs.at[s + 1, c], xs.at[s + 1, c], ag_s.at[s, d - 1], ag_r.at[s, d - 1],
+            xs.at[s + 1, c], xs.at[s + 1, c], ag_s.at[s], ag_r.at[s, d - 1],
             dev((c + d) % SEG, p),
         )
 
     def chain_back(s):
-        for d in range(1, SEG):
-            pltpu.make_async_copy(rs_in.at[s, d - 1], rs_in.at[s, d - 1], rs_r.at[s, d - 1]).wait()
+        pltpu.make_async_copy(rs_in.at[s], rs_in.at[s], rs_r.at[s]).wait()
         total = own_part[...]
         for d in range(1, SEG):
             total = total + rs_in[s, d - 1].astype(F32)
@@ -381,13 +439,11 @@
         for d in range(1, SEG):
             ag_copy(s, d).start()
 
-    middle = [[(1, 3), (2, 0)], [(2, 3), (3, 1)], [(3, 3)], []]
-    after = [[(1, 4), (2, 1), (3, 0), (2, 2)], [(2, 4), (3, 2)], [(3, 4)], []]
     for s in range(SEG):
         chain_front(s)
-        serve(middle[s])
+        serve(MIDDLE[s])
         chain_back(s)
-        serve(after[s])
+        serve(AFTER[s])
 
     for d in range(1, SEG):
         src = (c + SEG - d) % SEG
@@ -408,21 +464,17 @@
     for d in range(1, SEG):
         gain_copy(d).wait_send()
         qkg_copy(d).wait_send()
-    for dj in range(GROUP):
-        for dc in range(SEG):
-            if dc or dj:
-                stale_copy(dc, dj).wait_send()
-    for half in range(2):
-        spread_all(half, lambda copy: copy.wait_send())
+        stale_copy(d).wait_send()
+    stale_across().wait_send()
+    stale_mate().wait_send()
+    stale_mate_across().wait_send()
     for s in range(SEG):
-        for way, hops in ((0, LONG), (1, SHORT)):
-            for t in range(hops):
-                ring(s, t, way).wait_send()
-            for t in range(way, hops + 1):
-                to_mate(s, t, way).wait_send()
-        for d in range(1, SEG):
-            rs_copy(s, d).wait_send()
-            ag_copy(s, d).wait_send()
+        spread_all(s, lambda copy: copy.wait_send())
+    for s in range(SEG):
+        for block, sem in (
+            (w.at[s, core, pl.ds(0, NZ - 1)], ring_s), (w.at[s, core], m_s), (rs_out.at[s], rs_s), (rs_out.at[s], ag_s)
+        ):
+            pltpu.make_async_copy(block, block, sem.at[s]).wait()
 
 
 def per_device(x_in, stale_kv, owner, live, gain, qk_gain, w_qkv, w_out):
@@ -448,7 +500,7 @@
             pltpu.VMEM((SEG, 2, NZ, NY // 2, BLOCK, PIECE), BF),
             pltpu.VMEM((SEG, ROWS, PIECE), BF),
             pltpu.VMEM((SEG, GROUP, ROWS, PIECE), BF),
-            pltpu.VMEM((SEG, 1, D), F32),
+            pltpu.VMEM((SEG, SEG, 1, PIECE), F32),
             pltpu.VMEM((SEG, 2, HEAD), F32),
             pltpu.VMEM((SEG + 1, SEG, ROWS, PIECE), BF),
             pltpu.VMEM((SEG, SEG - 1, ROWS, PIECE), BF),
@@ -456,11 +508,10 @@
             pltpu.VMEM((ROWS, PIECE), F32),
             dma((6,)), dma((SEG, 2)), dma((2,)),
             dma((SEG - 1,)), dma((SEG - 1,)), dma((SEG - 1,)), dma((SEG - 1,)),
-            dma((SEG * GROUP,)), dma((SEG,)),
-            dma((2, NY)), dma((SEG,)),
-            dma((SEG, LONG)), dma((SEG, LONG)), dma((SEG, SHORT)), dma((SEG, SHORT)),
-            dma((SEG, NZ)), dma((SEG,)),
-            dma((SEG, SEG - 1)), dma((SEG, SEG - 1)), dma((SEG, SEG - 1)), dma((SEG, SEG - 1)),
+            dma((6,)), dma((SEG,)),
+            dma((2, NY)), dma((SEG, GROUP)),
+            dma((SEG,)), dma(((NZ - 1) * sum(PARTS),)), dma((SEG,)), dma((SEG,)),
+            dma((SEG,)), dma((SEG,)), dma((SEG,)), dma((SEG, SEG - 1)),
         ],
         compiler_params=pltpu.CompilerParams(
             collective_id=0, has_side_effects=True, vmem_limit_bytes=62 * 2**20

time: 97.3 us -> 92.9 us (0.955)
  the two profiles are of different devices: /device:TPU:6 before, /device:TPU:80 now
where the time goes in v3:
time: 92.9 us; the launch traced here: 92.7 us
  Pallas kernels  90.4 us (97%)
  local copies, waits for them, and re-layouts  1.62 us (2%)
    pallas_call x1, Pallas kernels, per_device(): pl.pallas_call(kernel, out_shape=jax.ShapeDtypeStruct((1, ROWS, D), BF),...  90.4 us

profile of v3, /device:TPU:80, one launch (start us, length us, event | category | flops | bytes accessed | tf_op | source)
XLA Modules:
  0.0 92.7 jit_solution(8834944910943275564)
XLA Ops:
  0.7 90.4 %shard_map.82 = bf16[1,64,1536]{2,1,0:T(8,128)(2,1)} custom-call(bf16[64,1536]{1,0:T(8,128)(2,1)} %x_hbm.1, bf16[64,1536]{1,0:T(8,128)(2,1)} %bitcast.7, s32[16,32]{1,0:T(8,128)} %bitcast.10, s32[1]{0:T(128)S(6)} %copy.10.live_ref, f32[1,1536]{1,0:T(1,128)} %gain_hbm.1, f32[2,64]{1,0:T(2,128)} %bitcast.11, bf16[12,2304]{1,0:T(8,128)(2,1)} %bitcast.8, ...), custom_call_target="tpu_custom_call" | custom-call | tf_op jit(solution)/shard_map/pallas_call | solution.py:485
  91.1 1.6 %copy.11 = bf16[1,64,1536]{2,1,0:T(8,128)(2,1)} copy(bf16[1,64,1536]{2,1,0:T(8,128)(2,1)} %shard_map.82) | data formatting | bytes 393216

commit v4 on v3

--- a/solution.py
+++ b/solution.py
@@ -30,9 +30,10 @@
 HD = 768
 LONG = NZ // 2
 PARTS = (2, 1, 1, 1)
-BEFORE = [(0, 0), (1, -1), (-1, 0), (0, 1), (0, 2), (1, 0), (2, -1), (0, 3), (-1, 1), (1, 1)]
-MIDDLE = [[(2, 0), (3, -1), (1, 2)], [(3, 0), (2, 2)], [(3, 2)], []]
-AFTER = [[(1, 3), (2, 1)], [(2, 3), (3, 1)], [(3, 3)], []]
+FIRST = [(0, -1), (1, -1)]
+BEFORE = [(0, 0), (-1, 0), (0, 1), (0, 2), (1, 0), (2, -1), (0, 3), (-1, 1), (1, 1)]
+MIDDLE = [[(-1, 2), (2, 0), (3, -1), (1, 2)], [(3, 0), (2, 2)], [(3, 2)], []]
+AFTER = [[(-1, 3), (1, 3), (2, 1)], [(2, 3), (3, 1)], [(3, 3)], []]
 
 
 def kernel(
@@ -115,7 +116,7 @@
             dev(g, image * GROUP + holder[piece]),
         )
 
-    for d in range(SEG):
+    for d in (2, 1, 3, 0):
         for piece in range(2):
             if d:
                 stage(d, piece).start()
@@ -148,17 +149,22 @@
         g = (c + d) % SEG
         return remote(stsend.at[g], st.at[c, j], st_s.at[d], st_r.at[0], dev(g, p))
 
-    def stale_across():
-        return remote(st.at[:, j], st.at[:, j], st_s.at[0], st_r.at[1], dev(c, across))
-
-    def stale_mate():
-        return remote(st.at[:, j], st.at[:, j], st_s.at[4], st_r.at[2], dev(c, mate))
-
-    def stale_mate_across():
-        return remote(st.at[:, j_across], st.at[:, j_across], st_s.at[5], st_r.at[3], dev(c, mate))
-
-    def stale_wait(n, index):
-        block = st.at[:, index]
+    def stale_rows(rest, index):
+        return st.at[pl.ds(1, SEG - 1), index] if rest else st.at[0, index]
+
+    def stale_across(rest):
+        block = stale_rows(rest, j)
+        return remote(block, block, st_s.at[4 + rest], st_r.at[1 + rest], dev(c, across))
+
+    def stale_mate(rest):
+        block = stale_rows(rest, j)
+        return remote(block, block, st_s.at[6 + rest], st_r.at[3 + rest], dev(c, mate))
+
+    def stale_mate_across(rest):
+        block = stale_rows(rest, j_across)
+        return remote(block, block, st_s.at[8 + rest], st_r.at[5 + rest], dev(c, mate))
+
+    def stale_wait(block, n):
         pltpu.make_async_copy(block, block, st_r.at[n]).wait()
 
     a = lax.broadcasted_iota(jnp.int32, (BLOCK, GROUP * SLOT), 0)
@@ -183,7 +189,7 @@
         else:
             target = patch_of((z + delta) % NZ, y, 1)
             dst, slot = w.at[s, 1, y, z % 4], z % 4
-        return remote(blk.at[half], dst, y_s.at[half, delta], y_r.at[s, slot], dev(c, target))
+        return remote(blk.at[half], dst, y_s.at[half, delta], y_r.at[s, slot // 2], dev(c, target))
 
     def spread_all(s, act):
         half = s // 2
@@ -193,7 +199,7 @@
             def _():
                 if s % 2 != piece:
                     act(spread(half, piece, 0))
-                for delta in (1, 7, 2, 6, 3, 5, 4):
+                for delta in (4, 3, 5, 2, 6, 1, 7):
                     act(spread(half, piece, delta))
 
     def spread_start(s):
@@ -202,13 +208,13 @@
 
             @pl.when((core == 0) & holds_a)
             def _():
-                pltpu.make_async_copy(blk.at[half], w.at[s, 0, z, yp], y_r.at[s, yp]).start()
+                pltpu.make_async_copy(blk.at[half], w.at[s, 0, z, yp], y_r.at[s, yp // 2]).start()
 
         else:
 
             @pl.when((core == 1) & jnp.logical_not(holds_a))
             def _():
-                pltpu.make_async_copy(blk.at[half], w.at[s, 1, y, z % 4], y_r.at[s, z % 4]).start()
+                pltpu.make_async_copy(blk.at[half], w.at[s, 1, y, z % 4], y_r.at[s, z % 4 // 2]).start()
 
         spread_all(s, lambda copy: copy.start())
 
@@ -251,9 +257,10 @@
         for q in range(PARTS[s]):
             block, part = ring_block(s, 0, 0, q)
             size = GROUP // PARTS[s]
-            for n in range(size):
-                one = w.at[s, core, place, part * size + n]
-                pltpu.make_async_copy(one, one, y_r.at[s, part * size + n]).wait()
+            for n in range(size // 2):
+                half = part * size // 2 + n
+                two = w.at[s, core, place, pl.ds(2 * half, 2)]
+                pltpu.make_async_copy(two, two, y_r.at[s, half]).wait()
             for step in (2, 1):
                 for way in range(2):
                     ring_copy(s, way, 0, step, q).start()
@@ -264,9 +271,9 @@
         for q in range(PARTS[s]):
             for way in range(2):
                 ring_wait(s, way, 2, q)
-                ring_copy(s, way, 2, 1, q).start()
                 if way == s % 2:
                     ring_copy(s, way, 2, 2, q).start()
+                ring_copy(s, way, 2, 1, q).start()
         for q in range(PARTS[s]):
             for way in range(2):
                 to_mate(s, way, 2, q).start()
@@ -279,13 +286,15 @@
                     to_mate(s, way, distance, q).start()
 
     def stale_step(n):
-        if n == 0:
-            stale_wait(0, j)
-            stale_across().start()
-            stale_mate().start()
+        rest = n // 2
+        if n % 2 == 0:
+            if rest == 0:
+                stale_wait(st.at[:, j], 0)
+            stale_across(rest).start()
+            stale_mate(rest).start()
         else:
-            stale_wait(1, j_across)
-            stale_mate_across().start()
+            stale_wait(stale_rows(rest, j_across), 1 + rest)
+            stale_mate_across(rest).start()
 
     def serve(plan):
         for s, t in plan:
@@ -301,7 +310,7 @@
                 ring_hand(s, (1,) if t == 2 else (3, 4))
 
     compact(0)
-    serve([(0, -1)])
+    serve(FIRST)
     for d in range(1, SEG):
         gain_copy(d).start()
         qkg_copy(d).start()
@@ -393,9 +402,9 @@
         key = head_norm(qk[:, GW:], jnp.concatenate([gk] * GH, 1)).astype(BF)
         query = query.astype(BF).astype(F32)
         stacked = jnp.concatenate([jnp.where(head_of[h], query, 0.0) for h in range(GH)], 0).astype(BF)
-        if s == 0:
-            stale_wait(2, j + 1 - 2 * core)
-            stale_wait(3, j_across + 1 - 2 * core)
+        if s < 2:
+            stale_wait(stale_rows(s, j + 1 - 2 * core), 3 + s)
+            stale_wait(stale_rows(s, j_across + 1 - 2 * core), 5 + s)
         kv = st[s].reshape(IMG, PIECE)
         scale = HEAD**-0.5
         far = jnp.exp(nt(stacked, kv[:, :GW]) * scale) * far_mask
@@ -430,14 +439,26 @@
             dev((c + d) % SEG, p),
         )
 
+    def last_copy():
+        return remote(
+            xs.at[SEG, c], xs.at[SEG, c], ag_s.at[SEG - 1], ag_r.at[SEG - 1, (2 * SEG - 2 - c) % SEG],
+            dev(SEG - 1, p),
+        )
+
     def chain_back(s):
         pltpu.make_async_copy(rs_in.at[s], rs_in.at[s], rs_r.at[s]).wait()
         total = own_part[...]
         for d in range(1, SEG):
             total = total + rs_in[s, d - 1].astype(F32)
         xs[s + 1, c] = (xs[s, c].astype(F32) + total).astype(BF)
-        for d in range(1, SEG):
-            ag_copy(s, d).start()
+        if s + 1 < SEG:
+            for d in (2, 1, 3):
+                ag_copy(s, d).start()
+        else:
+
+            @pl.when(c != SEG - 1)
+            def _():
+                last_copy().start()
 
     for s in range(SEG):
         chain_front(s)
@@ -445,9 +466,12 @@
         chain_back(s)
         serve(AFTER[s])
 
-    for d in range(1, SEG):
-        src = (c + SEG - d) % SEG
-        pltpu.make_async_copy(xs.at[SEG, src], xs.at[SEG, src], ag_r.at[SEG - 1, d - 1]).wait()
+    @pl.when(c == SEG - 1)
+    def _():
+        for d in range(1, SEG):
+            src = (c + SEG - d) % SEG
+            pltpu.make_async_copy(xs.at[SEG, src], xs.at[SEG, src], ag_r.at[SEG - 1, d - 1]).wait()
+
     for g in range(SEG):
         out_ref[0, :, g * PIECE : (g + 1) * PIECE] = xs[c + 1, g]
 
@@ -465,16 +489,22 @@
         gain_copy(d).wait_send()
         qkg_copy(d).wait_send()
         stale_copy(d).wait_send()
-    stale_across().wait_send()
-    stale_mate().wait_send()
-    stale_mate_across().wait_send()
+    for rest in range(2):
+        stale_across(rest).wait_send()
+        stale_mate(rest).wait_send()
+        stale_mate_across(rest).wait_send()
     for s in range(SEG):
         spread_all(s, lambda copy: copy.wait_send())
     for s in range(SEG):
         for block, sem in (
             (w.at[s, core, pl.ds(0, NZ - 1)], ring_s), (w.at[s, core], m_s), (rs_out.at[s], rs_s), (rs_out.at[s], ag_s)
         ):
-            pltpu.make_async_copy(block, block, sem.at[s]).wait()
+            if sem is not ag_s or s + 1 < SEG:
+                pltpu.make_async_copy(block, block, sem.at[s]).wait()
+
+    @pl.when(c != SEG - 1)
+    def _():
+        last_copy().wait_send()
 
 
 def per_device(x_in, stale_kv, owner, live, gain, qk_gain, w_qkv, w_out):
@@ -508,8 +538,8 @@
             pltpu.VMEM((ROWS, PIECE), F32),
             dma((6,)), dma((SEG, 2)), dma((2,)),
             dma((SEG - 1,)), dma((SEG - 1,)), dma((SEG - 1,)), dma((SEG - 1,)),
-            dma((6,)), dma((SEG,)),
-            dma((2, NY)), dma((SEG, GROUP)),
+            dma((10,)), dma((7,)),
+            dma((2, NY)), dma((SEG, 2)),
             dma((SEG,)), dma(((NZ - 1) * sum(PARTS),)), dma((SEG,)), dma((SEG,)),
             dma((SEG,)), dma((SEG,)), dma((SEG,)), dma((SEG, SEG - 1)),
         ],

time: 92.9 us -> 90 us (0.969)
  the two profiles are of different devices: /device:TPU:80 before, /device:TPU:6 now
where the time goes in v4:
time: 90 us; the launch traced here: 89.8 us
  Pallas kernels  87.5 us (97%)
  local copies, waits for them, and re-layouts  1.62 us (2%)
    pallas_call x1, Pallas kernels, per_device(): pl.pallas_call(kernel, out_shape=jax.ShapeDtypeStruct((1, ROWS, D), BF),...  87.5 us

profile of v4, /device:TPU:6, one launch (start us, length us, event | category | flops | bytes accessed | tf_op | source)
XLA Modules:
  0.0 89.8 jit_solution(9039995136203418855)
XLA Ops:
  0.7 87.5 %shard_map.82 = bf16[1,64,1536]{2,1,0:T(8,128)(2,1)} custom-call(bf16[64,1536]{1,0:T(8,128)(2,1)} %x_hbm.1, bf16[64,1536]{1,0:T(8,128)(2,1)} %bitcast.7, s32[16,32]{1,0:T(8,128)} %bitcast.10, s32[1]{0:T(128)S(6)} %copy.10.live_ref, f32[1,1536]{1,0:T(1,128)} %gain_hbm.1, f32[2,64]{1,0:T(2,128)} %bitcast.11, bf16[12,2304]{1,0:T(8,128)(2,1)} %bitcast.8, ...), custom_call_target="tpu_custom_call" | custom-call | tf_op jit(solution)/shard_map/pallas_call | solution.py:515
  88.2 1.6 %copy.11 = bf16[1,64,1536]{2,1,0:T(8,128)(2,1)} copy(bf16[1,64,1536]{2,1,0:T(8,128)(2,1)} %shard_map.82) | data formatting | bytes 393216

commit v5 on v4

--- a/solution.py
+++ b/solution.py
@@ -29,9 +29,9 @@
 D = 1536
 HD = 768
 LONG = NZ // 2
-PARTS = (2, 1, 1, 1)
+PARTS = (2, 2, 2, 2)
 FIRST = [(0, -1), (1, -1)]
-BEFORE = [(0, 0), (-1, 0), (0, 1), (0, 2), (1, 0), (2, -1), (0, 3), (-1, 1), (1, 1)]
+BEFORE = [(0, 0), (-1, 0), (0, 1), (1, 0), (0, 2), (2, -1), (0, 3), (-1, 1), (1, 1)]
 MIDDLE = [[(-1, 2), (2, 0), (3, -1), (1, 2)], [(3, 0), (2, 2)], [(3, 2)], []]
 AFTER = [[(-1, 3), (1, 3), (2, 1)], [(2, 3), (3, 1)], [(3, 3)], []]
 
@@ -75,6 +75,9 @@
 
     barrier = pltpu.get_barrier_semaphore()
     partners = []
+    for dz in range(1, NZ):
+        for low in range(2):
+            partners.append(dev(c, patch_of((z + dz) % NZ, y, low)))
     for dc in range(SEG):
         for dj in range(GROUP):
             if dc or dj:
@@ -83,9 +86,6 @@
         pair = (yp + dy) % (NY // 2)
         for low in range(4):
             partners.append(dev(c, z * (2 * NY) + pair * 4 + low))
-    for dz in range(1, NZ):
-        for low in range(2):
-            partners.append(dev(c, patch_of((z + dz) % NZ, y, low)))
     for partner in partners:
         pl.semaphore_signal(barrier, inc=1, device_id=partner, device_id_type=MESH)
 
@@ -323,7 +323,7 @@
                 :, part * HD + g * GW : part * HD + (g + 1) * GW
             ]
     pltpu.make_async_copy(stsend.at[c], st.at[c, j], st_r.at[0]).start()
-    for d in range(1, SEG):
+    for d in (2, 1, 3):
         stale_copy(d).start()
     inputs[5].wait()
     for g in range(SEG):

time: 90 us -> 89 us (0.989); the launches traced: 89.8 us -> 87.4 us
  Pallas kernels: 87.5 us -> 85.2 us
    pallas_call x1, Pallas kernels: 87.5 us -> 85.2 us  [per_device(): pl.pallas_call(kernel, out_shape=jax.ShapeDtypeStruct((1, ROWS, D), BF),...]
where the time goes in v5:
time: 89 us; the launch traced here: 87.4 us
  Pallas kernels  85.2 us (96%)
  local copies, waits for them, and re-layouts  1.62 us (2%)
    pallas_call x1, Pallas kernels, per_device(): pl.pallas_call(kernel, out_shape=jax.ShapeDtypeStruct((1, ROWS, D), BF),...  85.2 us

profile of v5, /device:TPU:6, one launch (start us, length us, event | category | flops | bytes accessed | tf_op | source)
XLA Modules:
  0.0 87.4 jit_solution(10891594615172060655)
XLA Ops:
  0.7 85.2 %shard_map.82 = bf16[1,64,1536]{2,1,0:T(8,128)(2,1)} custom-call(bf16[64,1536]{1,0:T(8,128)(2,1)} %x_hbm.1, bf16[64,1536]{1,0:T(8,128)(2,1)} %bitcast.7, s32[16,32]{1,0:T(8,128)} %bitcast.10, s32[1]{0:T(128)S(6)} %copy.10.live_ref, f32[1,1536]{1,0:T(1,128)} %gain_hbm.1, f32[2,64]{1,0:T(2,128)} %bitcast.11, bf16[12,2304]{1,0:T(8,128)(2,1)} %bitcast.8, ...), custom_call_target="tpu_custom_call" | custom-call | tf_op jit(solution)/shard_map/pallas_call | solution.py:515
  85.8 1.6 %copy.11 = bf16[1,64,1536]{2,1,0:T(8,128)(2,1)} copy(bf16[1,64,1536]{2,1,0:T(8,128)(2,1)} %shard_map.82) | data formatting | bytes 393216
